TPU v7x, 32 devices: a whole 2x2x4 slice. The times are simulated.
32 devices in a mesh: energy: 8 (over z, y), slab: 4 (over x, core).
Axes of the slice: x: 2, y: 2, z: 4, core: 2. Of those that a mesh axis runs over, the one named last changes fastest.
Arguments:
- lesser: bfloat16 [8, 4, 2, 1024, 1024], P('energy', 'slab'), may hold values from -6 to 6
- greater_diag: float32 [8, 4, 1024], P('energy', 'slab'), may hold values from -6 to 6
- dipole: bfloat16 [4, 1024, 1024], P('slab'), may hold values from -0.1875 to 0.1875
- photon_weights: float32 [8, 3], P('energy'), may hold values from 0.2 to 1
- sidebands: int32 [8], P('energy'), may hold values from 1 to 2
- phonon_lags: int32 [6], replicated, may hold values from 1 to 3
- phonon_strengths: float32 [2, 6], replicated, may hold values from 0.3 to 1.5
- slab_coupling: float32 [4, 1024], P('slab'), may hold values from 0.3 to 1
Outputs:
- lesser_self: bfloat16 [8, 4, 2, 1024, 1024], P('energy', 'slab')
- greater_phonon: float32 [8, 4, 1024], P('energy', 'slab')
All inputs are finite; a program needn't handle non-finite values.
Results may differ from a plain program's by a relative error of at most 0.0057.
Values may be sent and summed in bfloat16 or wider, within the bound.
No kernel may reach another device: no remote copies, remote signals or barrier semaphores. Data moves between devices by JAX's collectives and lax.ppermute only.
A program may use at most 64 MiB of HBM per device.

v0:
```python
import functools

import jax
import jax.numpy as jnp
from jax import lax
from jax.experimental import pallas as pl
from jax.experimental.pallas import tpu as pltpu
from jax.sharding import PartitionSpec as P

PHOT_BLOCKS = 3
CHUNKS = (((0, 0, 7),), ((1, 0, 2),), ((1, 2, 5),), ((1, 7, 1), (0, 7, 1)))
MIDDLE = ((1, 0, 7),)
EIGHTHS = 8
VMEM_BYTES = 20 * 1024 * 1024
EARLY_VMEM_BYTES = 53 * 1024 * 1024
FIRST_VMEM_BYTES = 48 * 1024 * 1024

STRAIGHT = ((0, 3), (2, 5), (3, 6), (4, 1), (5, 2), (7, 4))
CROSS = ((1, 4), (3, 0), (4, 7), (6, 3))
DETOURS = ((1, 0, 4), (6, 7, 3))
EDGES = ((3, 0), (4, 7))

TO_HUBS = ((3, 1), (4, 6))
BETWEEN_HUBS = ((1, 6), (6, 1))
FROM_HUBS = (((1, 3), (6, 4)), ((1, 5), (6, 2)), ((1, 7), (6, 0)))


def shifted(block, axis, distance):
    devices = range(lax.axis_size(axis))
    return lax.ppermute(
        block, axis, [(i - distance, i) for i in devices if i - distance in devices]
    )


def any_of(own, energies):
    return functools.reduce(jnp.logical_or, [own == energy for energy in energies])


def side_weight(own, route, low, high):
    from_low = any_of(own, [target for source, target in route if source < target])
    from_high = any_of(own, [target for source, target in route if source > target])
    return jnp.where(from_low, low, jnp.where(from_high, high, 0.0))


def doubled(block, axis, step):
    other = lax.ppermute(block, axis, [(i, i ^ step) for i in range(lax.axis_size(axis))])
    upper = (lax.axis_index(axis) & step) != 0
    return jnp.concatenate(
        [jnp.where(upper, other, block), jnp.where(upper, block, other)], axis=0
    )


def diagonals_body(tile, lesser_ref, greater_ref, out_ref, tiles, arrived):
    count = tiles.shape[0]
    copies = [
        pltpu.make_async_copy(
            lesser_ref.at[0, 0, 1, pl.ds(n * tile, tile), pl.ds(n * tile, tile)],
            tiles.at[n],
            arrived.at[n],
        )
        for n in range(count)
    ]
    for copy in copies:
        copy.start()
    row = lax.broadcasted_iota(jnp.int32, (tile, tile), 0)
    col = lax.broadcasted_iota(jnp.int32, (tile, tile), 1)
    out_ref[0, 1:2] = greater_ref[0]
    for n, copy in enumerate(copies):
        copy.wait()
        block = jnp.where(row == col, tiles[n].astype(jnp.float32), 0.0)
        out_ref[0, 0:1, n * tile : (n + 1) * tile] = jnp.sum(block, axis=0, keepdims=True)


def diagonals_of(lesser, greater_diag):
    width = lesser.shape[-1]
    tile = 128
    return pl.pallas_call(
        functools.partial(diagonals_body, tile),
        in_specs=[
            pl.BlockSpec(memory_space=pltpu.HBM),
            pl.BlockSpec(memory_space=pltpu.VMEM),
        ],
        out_specs=pl.BlockSpec(memory_space=pltpu.VMEM),
        out_shape=jax.ShapeDtypeStruct((1, 2, width), jnp.float32),
        scratch_shapes=[
            pltpu.VMEM((width // tile, tile, tile), lesser.dtype),
            pltpu.SemaphoreType.DMA((width // tile,)),
        ],
        compiler_params=pltpu.CompilerParams(vmem_limit_bytes=EARLY_VMEM_BYTES),
        name="diagonals",
    )(lesser, greater_diag)


def lag_kernel(rows, cols, phonon_lags, first, second):
    offset = cols[None, :] - rows[:, None]
    upward = (offset[None, :, :] == phonon_lags[:, None, None]).astype(jnp.float32)
    downward = (offset[None, :, :] == -phonon_lags[:, None, None]).astype(jnp.float32)
    return jnp.sum(first[:, None, None] * upward + second[:, None, None] * downward, axis=0)


def left_body(chunk, streamed, lesser_ref, dipole_ref, left_ref, *scratch):
    width = left_ref.shape[0]
    unit, rows = width // EIGHTHS, width // 4
    starts = range(0, width, rows)
    if streamed:
        blocks, arrived = scratch
        copies = [
            pltpu.make_async_copy(
                lesser_ref.at[0, 0, chunk[0][0], pl.ds(i, rows)], blocks.at[pl.ds(i, rows)], sem
            )
            for i, sem in zip(starts, [arrived.at[n] for n in range(len(starts))])
        ]
        for copy in copies:
            copy.start()
    at = 0
    for part, first, eighths in chunk:
        cols = eighths * unit
        for n, i in enumerate(starts):
            if streamed:
                copies[n].wait()
                block = blocks[i : i + rows]
            else:
                block = lesser_ref[0, 0, part, i : i + rows]
            left_ref[i : i + rows, at : at + cols] = lax.dot_general(
                block,
                dipole_ref[0, first * unit : first * unit + cols],
                (((1,), (1,)), ((), ())),
                preferred_element_type=jnp.float32,
            ).astype(left_ref.dtype)
        at += cols


def left_of(lesser, dipole, chunk, streamed=False):
    width = lesser.shape[-1]
    cols = width // EIGHTHS * sum(eighths for _, _, eighths in chunk)
    scratch = [pltpu.VMEM((width, width), lesser.dtype), pltpu.SemaphoreType.DMA((4,))]
    return pl.pallas_call(
        functools.partial(left_body, chunk, streamed),
        in_specs=[
            pl.BlockSpec(memory_space=pl.ANY if streamed else pltpu.VMEM),
            pl.BlockSpec(memory_space=pltpu.VMEM),
        ],
        out_specs=pl.BlockSpec(memory_space=pltpu.VMEM),
        out_shape=jax.ShapeDtypeStruct((width, cols), lesser.dtype),
        scratch_shapes=scratch if streamed else [],
        compiler_params=pltpu.CompilerParams(
            vmem_limit_bytes=FIRST_VMEM_BYTES if streamed else VMEM_BYTES
        ),
        name="left",
    )(lesser, dipole)


def either_body(flag_ref, yes_ref, no_ref, out_ref):
    height = out_ref.shape[0]
    rows = height // 16

    def copied_from(ref):
        @pl.loop(0, height // rows)
        def _(i):
            at = pl.ds(pl.multiple_of(i * rows, rows), rows)
            out_ref[at] = ref[at]

    pl.when(flag_ref[0] != 0)(lambda: copied_from(yes_ref))
    pl.when(flag_ref[0] == 0)(lambda: copied_from(no_ref))


def either_of(flag, yes, no):
    return pl.pallas_call(
        either_body,
        in_specs=[
            pl.BlockSpec(memory_space=pltpu.SMEM),
            pl.BlockSpec(memory_space=pltpu.VMEM),
            pl.BlockSpec(memory_space=pltpu.VMEM),
        ],
        out_specs=pl.BlockSpec(memory_space=pltpu.VMEM),
        out_shape=jax.ShapeDtypeStruct(yes.shape, yes.dtype),
        compiler_params=pltpu.CompilerParams(vmem_limit_bytes=VMEM_BYTES),
        name="either",
    )(flag.astype(jnp.int32).reshape(1), yes, no)


def held_body(block_ref, out_ref):
    out_ref[...] = block_ref[...]


def held_of(block):
    return pl.pallas_call(
        held_body,
        in_specs=[pl.BlockSpec(memory_space=pltpu.VMEM)],
        out_specs=pl.BlockSpec(memory_space=pltpu.VMEM),
        out_shape=jax.ShapeDtypeStruct(block.shape, block.dtype),
        cost_estimate=pl.CostEstimate(flops=4000000000, bytes_accessed=0, transcendentals=0),
        compiler_params=pltpu.CompilerParams(vmem_limit_bytes=VMEM_BYTES),
        name="held",
    )(block)


def pieces_of(chunk):
    pieces, place = [], 0
    for part, first, eighths in chunk:
        for at in range(first, first + eighths, 2):
            size = min(2, first + eighths - at)
            pieces.append((part, at, place, size))
            place += size
    return pieces


def photon_body(chunk, skips, factors_ref, dipole_ref, phonon_ref, own_ref, *rest):
    sides, (out_ref, results, sent) = rest[: len(skips)], rest[-3:]
    width = own_ref.shape[0]
    unit = width // EIGHTHS
    factors = [factors_ref[n] for n in range(2 + len(skips))]
    copies = []
    for k, (part, at, place, size) in enumerate(pieces_of(chunk)):
        at, place, cols = at * unit, place * unit, size * unit

        def piece(ref, skip=0):
            return ref[:, skip * unit + place : skip * unit + place + cols].astype(jnp.float32)

        side = factors[2] * piece(sides[0], skips[0])
        for factor, ref, skip in zip(factors[3:], sides[1:], skips[1:]):
            side += factor * piece(ref, skip)
        mixed = (factors[0] * piece(own_ref) + factors[1] * side).astype(jnp.bfloat16)
        photon = jnp.dot(dipole_ref[0], mixed, preferred_element_type=jnp.float32)
        if part == 1:
            row = lax.broadcasted_iota(jnp.int32, photon.shape, 0)
            col = lax.broadcasted_iota(jnp.int32, photon.shape, 1) + at
            photon += jnp.where(row == col, phonon_ref[:, at : at + cols], 0.0)
        results[k, :, :cols] = photon.astype(results.dtype)
        copies.append(
            pltpu.make_async_copy(
                results.at[k, :, pl.ds(0, cols)],
                out_ref.at[0, 0, part, :, pl.ds(at, cols)],
                sent.at[k],
            )
        )
        copies[-1].start()
    for copy in copies:
        copy.wait()


def photon_of(chunk, factors, dipole, phonon, own, sides, out):
    width = own.shape[0]
    sides, skips = zip(*sides)
    n_pieces = len(pieces_of(chunk))
    operands = [factors, dipole, phonon, own, *sides]
    in_specs = [pl.BlockSpec(memory_space=pltpu.SMEM)]
    in_specs += [pl.BlockSpec(memory_space=pltpu.VMEM)] * (len(operands) - 1)
    aliases = {}
    if out is not None:
        aliases = {len(operands): 0}
        operands.append(out)
        in_specs.append(pl.BlockSpec(memory_space=pl.ANY))
    return pl.pallas_call(
        functools.partial(photon_body, chunk, skips),
        in_specs=in_specs,
        out_specs=pl.BlockSpec(memory_space=pl.ANY),
        out_shape=jax.ShapeDtypeStruct((1, 1, 2, width, width), jnp.bfloat16),
        scratch_shapes=[
            pltpu.VMEM((n_pieces, width, 2 * width // EIGHTHS), jnp.bfloat16),
            pltpu.SemaphoreType.DMA((n_pieces,)),
        ],
        input_output_aliases=aliases,
        compiler_params=pltpu.CompilerParams(vmem_limit_bytes=VMEM_BYTES),
        name="photon",
    )(*operands)


def on_device(
    lesser,
    greater_diag,
    dipole,
    photon_weights,
    sidebands,
    phonon_lags,
    phonon_strengths,
    slab_coupling,
):
    e_count = lesser.shape[0]
    width = lesser.shape[-1]
    count = lax.axis_size("energy")
    own = lax.axis_index("energy")
    everyone = doubled(diagonals_of(lesser, greater_diag), "energy", 1)
    left = [left_of(lesser, dipole, CHUNKS[0], streamed=True)]
    left += [left_of(lesser, dipole, chunk) for chunk in CHUNKS[1:]]
    everyone, left[0] = lax.optimization_barrier((everyone, left[0]))
    weight_0, weight_low, weight_high = photon_weights[0]
    flag = sidebands[0].astype(jnp.float32)
    if count == 8:
        first, second = {}, {}
        hops = tuple((source, by) for source, by, _ in DETOURS)
        second_hops = tuple((by, target) for _, by, target in DETOURS)
        first[0] = lax.ppermute(left[0], "energy", STRAIGHT + hops)
        first[1] = lax.ppermute(left[1], "energy", STRAIGHT)

        is_low = own < count // 2
        for route in (TO_HUBS, BETWEEN_HUBS):
            other = lax.ppermute(everyone, "energy", route)
            everyone = jnp.concatenate(
                [jnp.where(is_low, everyone, other), jnp.where(is_low, other, everyone)], axis=0
            )
        held = jnp.where(any_of(own, [hub for hub, _ in BETWEEN_HUBS]), everyone, 0.0)
        for route in FROM_HUBS:
            held += lax.ppermute(everyone, "energy", route)
        everyone = held

        middle = left_of(lesser, dipole, MIDDLE)
        first[0], everyone, *left, middle = lax.optimization_barrier(
            (first[0], everyone, *left, middle)
        )
        relays = any_of(own, [by for by, _ in second_hops])
        onward = either_of(relays, first[0], left[0])
        second[0] = lax.ppermute(onward, "energy", EDGES + second_hops)
        crossed = lax.ppermute(middle, "energy", CROSS)
        first[2] = lax.ppermute(left[2], "energy", STRAIGHT)
        first[1] = held_of(first[1])
        first[1], left[3] = lax.optimization_barrier((first[1], left[3]))
        second[3] = lax.ppermute(left[3], "energy", CROSS)
        first[3] = lax.ppermute(left[3], "energy", STRAIGHT)
        weights = [
            side_weight(own, STRAIGHT, weight_low, weight_high),
            side_weight(own, CROSS, weight_low, weight_high),
        ]
    else:
        step = 2
        while step < count:
            everyone = doubled(everyone, "energy", step)
            step *= 2
        first = [shifted(block, "energy", PHOT_BLOCKS) for block in left]
        second = [shifted(block, "energy", -PHOT_BLOCKS) for block in left]
        weights = [weight_low, weight_high]
    factors = jnp.stack([weight_0, flag, *weights])
    if count == 8:
        sides = [
            [(first[0], 0), (second[0], 0)],
            [(first[1], 0), (crossed, 0)],
            [(first[2], 0), (crossed, 2)],
            [(first[3], 0), (second[3], 0)],
        ]
    else:
        sides = [[(low, 0), (high, 0)] for low, high in zip(first, second)]

    own_rows = own * e_count + jnp.arange(e_count, dtype=jnp.int32)
    all_rows = jnp.arange(e_count * count, dtype=jnp.int32)
    k_less = lag_kernel(own_rows, all_rows, phonon_lags, phonon_strengths[0], phonon_strengths[1])
    k_great = lag_kernel(own_rows, all_rows, phonon_lags, phonon_strengths[1], phonon_strengths[0])
    corr_less = jnp.sum(k_less[0][:, None] * everyone[:, 0], axis=0)
    corr_great = jnp.sum(k_great[0][:, None] * everyone[:, 1], axis=0)
    correlated = jnp.stack([corr_less, corr_great])
    below = shifted(slab_coupling * correlated, "slab", 1)
    above = shifted(correlated, "slab", -1)
    phon_less, phon_great = correlated + below + slab_coupling * above

    out = None
    for n, chunk in enumerate(CHUNKS):
        out = photon_of(chunk, factors, dipole, phon_less[None], left[n], sides[n], out)
    return out, phon_great[None, None]


def solution(mesh):
    return jax.shard_map(
        on_device,
        mesh=mesh,
        in_specs=(
            P("energy", "slab", None, None, None),
            P("energy", "slab", None),
            P("slab", None, None),
            P("energy", None),
            P("energy"),
            P(),
            P(),
            P("slab", None),
        ),
        out_specs=(P("energy", "slab", None, None, None), P("energy", "slab", None)),
        check_vma=False,
    )
```

profile of v0, /device:TPU:0, one launch (start us, length us, event | category | flops | bytes accessed | tf_op | source)
XLA Modules:
  0.0 158.4 jit_solution(17120401076564690155)
XLA Ops:
  0.6 0.8 copy-done.9
  1.5 1.0 diagonals.1
  2.5 3.0 %collective-permute-start = (f32[1,2,1024]{2,1,0:T(2,128)S(1)}, f32[1,2,1024]{2,1,0:T(2,128)S(1)}, u32[]{:S(2)}, u32[]{:S(2)}) collective-permute-start(f32[1,2,1024]{2,1,0:T(2,128)S(1)} %diagonals.1), channel_id=1, source_target_pairs={{0,4},{4,0},{8,12},{12,8},{16,20},{20,16},{24,28},{28,24},{1,5},{5... | collective-permute-start | bytes 24584 | tf_op jit(solution)/shard_map/ppermute | solution.py:46
  5.6 4.0 %left.5.no_ref.own_ref = bf16[1024,896]{1,0:T(8,128)(2,1)S(1)} custom-call(bf16[1,1,2,1024,1024]{4,3,2,1,0:T(8,128)(2,1)} %lesser_ref.11, bf16[1,1024,1024]{2,1,0:T(8,128)(2,1)S(1)} %copy-done), custom_call_target="tpu_custom_call" | custom-call | tf_op jit(solution)/shard_map/left/pallas_call | solution.py:137
  9.6 1.2 copy-done.3
  10.8 0.0 collective-permute-done
  10.8 0.0 copy-start.11
  10.9 1.6 collective-permute-start.1
  12.4 0.7 collective-permute-start.2
  13.1 0.0 copy-start.1
  13.1 2.2 %copy-done.1 = bf16[1,1,2,1024,1024]{4,3,2,1,0:T(8,128)(2,1)S(1)} copy-done((bf16[1,1,2,1024,1024]{4,3,2,1,0:T(8,128)(2,1)S(1)}, bf16[1,1,2,1024,1024]{4,3,2,1,0:T(8,128)(2,1)}, u32[]{:S(2)}) %copy-start.1) | copy-done | bytes 4194328
  15.3 1.6 left.6.own_ref
  16.8 6.9 %collective-permute-start.9 = (bf16[1024,256]{1,0:T(8,128)(2,1)}, bf16[1024,256]{1,0:T(8,128)(2,1)}, u32[]{:S(2)}, u32[]{:S(2)}) collective-permute-start(bf16[1024,256]{1,0:T(8,128)(2,1)} %left.6.own_ref), channel_id=1, source_target_pairs={{0,12},{8,20},{12,24},{16,4},{20,8},{28,16},{1,13},{9,21},{13,25},... | collective-permute-start | bytes 1572872 | tf_op jit(solution)/shard_map/ppermute | solution.py:294
  23.7 0.0 collective-permute-done.2
  23.7 0.7 collective-permute-start.3
  24.4 0.6 fusion.7
  25.0 2.2 %copy-done.2 = bf16[1,1,2,1024,1024]{4,3,2,1,0:T(8,128)(2,1)S(1)} copy-done((bf16[1,1,2,1024,1024]{4,3,2,1,0:T(8,128)(2,1)S(1)}, bf16[1,1,2,1024,1024]{4,3,2,1,0:T(8,128)(2,1)}, u32[]{:S(2)}) %copy-start.2) | copy-done | bytes 4194328
  27.2 2.4 %left.9 = bf16[1024,896]{1,0:T(8,128)(2,1)S(1)} custom-call(bf16[1,1,2,1024,1024]{4,3,2,1,0:T(8,128)(2,1)S(1)} %copy-done.2, bf16[1,1024,1024]{2,1,0:T(8,128)(2,1)S(1)} %copy-done), custom_call_target="tpu_custom_call" | custom-call | tf_op jit(solution)/shard_map/left/pallas_call | solution.py:137
  29.6 0.0 copy-start.7
  29.6 1.2 copy-done.7
  30.8 1.8 %left.7.own_ref = bf16[1024,640]{1,0:T(8,128)(2,1)S(1)} custom-call(bf16[1,1,2,1024,1024]{4,3,2,1,0:T(8,128)(2,1)S(1)} %copy-done.2, bf16[1,1024,1024]{2,1,0:T(8,128)(2,1)S(1)} %copy-done), custom_call_target="tpu_custom_call" | custom-call | tf_op jit(solution)/shard_map/left/pallas_call | solution.py:137
  32.6 0.0 copy-start.13
  32.7 1.2 left.8.own_ref
  33.9 0.8 copy-done.5
  34.7 0.0 copy-done.13
  37.8 0.0 collective-permute-done.3
  37.9 0.7 collective-permute-start.4
  38.6 0.7 collective-permute-start.5
  39.3 1.3 collective-permute-start.6
  40.6 0.0 collective-permute-done.4
  40.6 0.0 collective-permute-done.5
  40.6 6.7 %collective-permute-done.6 = f32[8,2,1024]{2,1,0:T(2,128)S(1)} collective-permute-done((f32[8,2,1024]{2,1,0:T(2,128)S(1)}, f32[8,2,1024]{2,1,0:T(2,128)S(1)}, u32[]{:S(2)}, u32[]{:S(2)}) %collective-permute-start.6) | collective-permute-done | bytes 65568 | tf_op jit(solution)/shard_map/ppermute | solution.py:304
  47.3 0.1 add_add_fusion
  47.4 5.8 %collective-permute-done.1.yes_ref.rest_0_ = bf16[1024,896]{1,0:T(8,128)(2,1)} collective-permute-done((bf16[1024,896]{1,0:T(8,128)(2,1)}, bf16[1024,896]{1,0:T(8,128)(2,1)}, u32[]{:S(2)}, u32[]{:S(2)}) %collective-permute-start.1) | collective-permute-done | bytes 1835040 | tf_op jit(solution)/shard_map/ppermute | solution.py:293
  53.2 1.5 copy-done.4
  54.7 1.8 %either.1 = bf16[1024,896]{1,0:T(8,128)(2,1)S(1)} custom-call(s32[1]{0:T(128)} %bitcast.10.flag_ref, bf16[1024,896]{1,0:T(8,128)(2,1)} %collective-permute-done.1.yes_ref.rest_0_, bf16[1024,896]{1,0:T(8,128)(2,1)S(1)} %copy-done.4), custom_call_target="tpu_custom_call" | custom-call | tf_op jit(solution)/shard_map/either/pallas_call | solution.py:168
  56.5 6.4 %collective-permute-start.14 = (bf16[1024,896]{1,0:T(8,128)(2,1)S(1)}, bf16[1024,896]{1,0:T(8,128)(2,1)S(1)}, u32[]{:S(2)}, u32[]{:S(2)}) collective-permute-start(bf16[1024,896]{1,0:T(8,128)(2,1)S(1)} %either.1), channel_id=1, source_target_pairs={{12,0},{16,28},{0,16},{28,12},{13,1},{17,29},{1,17},{29,13},{14,2}... | collective-permute-start | bytes 5505032 | tf_op jit(solution)/shard_map/ppermute | solution.py:313
  63.0 0.0 copy-done.8
  63.0 1.3 collective-permute-start.13
  64.3 0.0 copy-done.12
  64.3 0.1 fusion.5
  64.4 5.5 %collective-permute-start.12 = (bf16[1024,640]{1,0:T(8,128)(2,1)S(1)}, bf16[1024,640]{1,0:T(8,128)(2,1)S(1)}, u32[]{:S(2)}, u32[]{:S(2)}) collective-permute-start(bf16[1024,640]{1,0:T(8,128)(2,1)S(1)} %left.7.own_ref), channel_id=1, source_target_pairs={{0,12},{8,20},{12,24},{16,4},{20,8},{28,16},{1,13},{9,21},{13,25},... | collective-permute-start | bytes 3932168 | tf_op jit(solution)/shard_map/ppermute | solution.py:315
  70.0 0.1 fusion.6
  70.0 0.1 fusion
  70.2 1.3 collective-permute-start.7
  71.4 0.0 collective-permute-done.9.block_ref
  71.5 1.4 collective-permute-start.8
  72.9 1.1 held.1.rest_0_
  74.0 0.0 collective-permute-done.7
  74.0 0.0 copy-done.6
  74.0 41.3 %collective-permute-start.10 = (bf16[1024,256]{1,0:T(8,128)(2,1)S(1)}, bf16[1024,256]{1,0:T(8,128)(2,1)S(1)}, u32[]{:S(2)}, u32[]{:S(2)}) collective-permute-start(bf16[1024,256]{1,0:T(8,128)(2,1)S(1)} %copy-done.6), channel_id=1, source_target_pairs={{0,12},{8,20},{12,24},{16,4},{20,8},{28,16},{1,13},{9,21},{13,25},... | collective-permute-start | bytes 1572872 | tf_op jit(solution)/shard_map/ppermute | solution.py:319
  115.3 0.0 collective-permute-done.8
  115.3 1.5 collective-permute-start.11
  116.8 0.7 pad_maximum_fusion.4.factors_ref
  117.5 0.6 slice_bitcast_fusion
  118.1 0.0 collective-permute-done.14.rest_1_
  118.1 5.0 %photon.4.rest_2_ = bf16[1,1,2,1024,1024]{4,3,2,1,0:T(8,128)(2,1)} custom-call(f32[4]{0:T(128)S(1)} %pad_maximum_fusion.4.factors_ref, bf16[1,1024,1024]{2,1,0:T(8,128)(2,1)S(1)} %copy-done, f32[1,1024]{1,0:T(1,128)S(1)} %get-tuple-element.35.phonon_ref, bf16[1024,896]{1,0:T(8,128)(2,1)S(1)} %copy-done.4, ...), custom_call_target="tpu_custom_call" | custom-call | tf_op jit(solution)/shard_map/photon/pallas_call | solution.py:254
  123.1 22.6 %collective-permute-done.13.rest_1_ = bf16[1024,896]{1,0:T(8,128)(2,1)S(1)} collective-permute-done((bf16[1024,896]{1,0:T(8,128)(2,1)S(1)}, bf16[1024,896]{1,0:T(8,128)(2,1)S(1)}, u32[]{:S(2)}, u32[]{:S(2)}) %collective-permute-start.13) | collective-permute-done | bytes 1835040 | tf_op jit(solution)/shard_map/ppermute | solution.py:314
  145.7 2.7 %photon.5.rest_2_ = bf16[1,1,2,1024,1024]{4,3,2,1,0:T(8,128)(2,1)} custom-call(f32[4]{0:T(128)S(1)} %pad_maximum_fusion.4.factors_ref, bf16[1,1024,1024]{2,1,0:T(8,128)(2,1)S(1)} %copy-done, f32[1,1024]{1,0:T(1,128)S(1)} %get-tuple-element.35.phonon_ref, bf16[1024,256]{1,0:T(8,128)(2,1)} %left.6.own_ref, ...), custom_call_target="tpu_custom_call", output_to_operand_aliasing={{}: (6, {})} | custom-call | tf_op jit(solution)/shard_map/photon/pallas_call | solution.py:254
  148.5 0.0 collective-permute-done.12.rest_0_
  148.5 3.4 %photon.6.rest_2_ = bf16[1,1,2,1024,1024]{4,3,2,1,0:T(8,128)(2,1)} custom-call(f32[4]{0:T(128)S(1)} %pad_maximum_fusion.4.factors_ref, bf16[1,1024,1024]{2,1,0:T(8,128)(2,1)S(1)} %copy-done, f32[1,1024]{1,0:T(1,128)S(1)} %get-tuple-element.35.phonon_ref, bf16[1024,640]{1,0:T(8,128)(2,1)S(1)} %left.7.own_ref, ...), custom_call_target="tpu_custom_call", output_to_operand_aliasing={{}: (6, {})} | custom-call | tf_op jit(solution)/shard_map/photon/pallas_call | solution.py:254
  151.9 3.6 %collective-permute-done.10.rest_0_ = bf16[1024,256]{1,0:T(8,128)(2,1)S(1)} collective-permute-done((bf16[1024,256]{1,0:T(8,128)(2,1)S(1)}, bf16[1024,256]{1,0:T(8,128)(2,1)S(1)}, u32[]{:S(2)}, u32[]{:S(2)}) %collective-permute-start.10) | collective-permute-done | bytes 524320 | tf_op jit(solution)/shard_map/ppermute | solution.py:319
  155.5 0.0 collective-permute-done.11.rest_1_
  155.5 2.7 %photon.7 = bf16[1,1,2,1024,1024]{4,3,2,1,0:T(8,128)(2,1)} custom-call(f32[4]{0:T(128)S(1)} %pad_maximum_fusion.4.factors_ref, bf16[1,1024,1024]{2,1,0:T(8,128)(2,1)S(1)} %copy-done, f32[1,1024]{1,0:T(1,128)S(1)} %get-tuple-element.35.phonon_ref, bf16[1024,256]{1,0:T(8,128)(2,1)S(1)} %copy-done.6, ...), custom_call_target="tpu_custom_call", output_to_operand_aliasing={{}: (6, {})} | custom-call | tf_op jit(solution)/shard_map/photon/pallas_call | solution.py:254
  (24 shorter events, 0.2 us)
Async XLA Ops:
  0.6 4.9 %copy-start = (bf16[1,1024,1024]{2,1,0:T(8,128)(2,1)S(1)}, bf16[1,1024,1024]{2,1,0:T(8,128)(2,1)}, u32[]{:S(2)}) copy-start(bf16[1,1024,1024]{2,1,0:T(8,128)(2,1)} %dipole_ref.17) | copy-start | bytes 6291460
  0.6 0.8 copy-start.9
  2.5 8.3 %collective-permute-start = (f32[1,2,1024]{2,1,0:T(2,128)S(1)}, f32[1,2,1024]{2,1,0:T(2,128)S(1)}, u32[]{:S(2)}, u32[]{:S(2)}) collective-permute-start(f32[1,2,1024]{2,1,0:T(2,128)S(1)} %diagonals.1), channel_id=1, source_target_pairs={{0,4},{4,0},{8,12},{12,8},{16,20},{20,16},{24,28},{28,24},{1,5},{5... | collective-permute-start | bytes 24584 | tf_op jit(solution)/shard_map/ppermute | solution.py:46
  9.6 1.2 copy-start.3
  10.8 13.6 %copy-start.11 = (f32[1,3]{1,0:T(1,128)S(1)}, f32[1,3]{1,0:T(1,128)}, u32[]{:S(2)}) copy-start(f32[1,3]{1,0:T(1,128)} %param.11) | copy-start | bytes 40
  10.9 42.3 %collective-permute-start.1 = (bf16[1024,896]{1,0:T(8,128)(2,1)}, bf16[1024,896]{1,0:T(8,128)(2,1)}, u32[]{:S(2)}, u32[]{:S(2)}) collective-permute-start(bf16[1024,896]{1,0:T(8,128)(2,1)} %copy-done.3), channel_id=1, source_target_pairs={{0,12},{8,20},{12,24},{16,4},{20,8},{28,16},{4,0},{24,28},{1,13},{... | collective-permute-start | bytes 5505032 | tf_op jit(solution)/shard_map/ppermute | solution.py:293
  12.4 11.3 %collective-permute-start.2 = (f32[2,2,1024]{2,1,0:T(2,128)S(1)}, f32[2,2,1024]{2,1,0:T(2,128)S(1)}, u32[]{:S(2)}, u32[]{:S(2)}) collective-permute-start(f32[2,2,1024]{2,1,0:T(2,128)S(1)} %pad_maximum_fusion.2), channel_id=1, source_target_pairs={{12,4},{16,24},{13,5},{17,25},{14,6},{18,26},{15,7},{19,27}} | collective-permute-start | bytes 49160 | tf_op jit(solution)/shard_map/ppermute | solution.py:298
  13.1 2.2 %copy-start.1 = (bf16[1,1,2,1024,1024]{4,3,2,1,0:T(8,128)(2,1)S(1)}, bf16[1,1,2,1024,1024]{4,3,2,1,0:T(8,128)(2,1)}, u32[]{:S(2)}) copy-start(bf16[1,1,2,1024,1024]{4,3,2,1,0:T(8,128)(2,1)} %lesser_ref.11) | copy-start | bytes 12582916
  16.8 54.6 %collective-permute-start.9 = (bf16[1024,256]{1,0:T(8,128)(2,1)}, bf16[1024,256]{1,0:T(8,128)(2,1)}, u32[]{:S(2)}, u32[]{:S(2)}) collective-permute-start(bf16[1024,256]{1,0:T(8,128)(2,1)} %left.6.own_ref), channel_id=1, source_target_pairs={{0,12},{8,20},{12,24},{16,4},{20,8},{28,16},{1,13},{9,21},{13,25},... | collective-permute-start | bytes 1572872 | tf_op jit(solution)/shard_map/ppermute | solution.py:294
  23.7 14.1 %collective-permute-start.3 = (f32[4,2,1024]{2,1,0:T(2,128)S(1)}, f32[4,2,1024]{2,1,0:T(2,128)S(1)}, u32[]{:S(2)}, u32[]{:S(2)}) collective-permute-start(f32[4,2,1024]{2,1,0:T(2,128)S(1)} %pad_maximum_fusion.1), channel_id=1, source_target_pairs={{4,24},{24,4},{5,25},{25,5},{6,26},{26,6},{7,27},{27,7}} | collective-permute-start | bytes 98312 | tf_op jit(solution)/shard_map/ppermute | solution.py:298
  25.0 2.2 %copy-start.2 = (bf16[1,1,2,1024,1024]{4,3,2,1,0:T(8,128)(2,1)S(1)}, bf16[1,1,2,1024,1024]{4,3,2,1,0:T(8,128)(2,1)}, u32[]{:S(2)}) copy-start(bf16[1,1,2,1024,1024]{4,3,2,1,0:T(8,128)(2,1)} %lesser_ref.11) | copy-start | bytes 12582916
  29.6 1.2 copy-start.7
  32.6 2.1 %copy-start.13 = (s32[6]{0:T(128)S(1)}, s32[6]{0:T(128)}, u32[]{:S(2)}) copy-start(s32[6]{0:T(128)} %param.13) | copy-start | bytes 76
  33.9 0.8 copy-start.5
  37.9 2.7 %collective-permute-start.4 = (f32[8,2,1024]{2,1,0:T(2,128)S(1)}, f32[8,2,1024]{2,1,0:T(2,128)S(1)}, u32[]{:S(2)}, u32[]{:S(2)}) collective-permute-start(f32[8,2,1024]{2,1,0:T(2,128)S(1)} %pad_maximum_fusion), channel_id=1, source_target_pairs={{4,12},{24,16},{5,13},{25,17},{6,14},{26,18},{7,15},{27,19}} | collective-permute-start | bytes 196616 | tf_op jit(solution)/shard_map/ppermute | solution.py:304
  38.6 2.0 %collective-permute-start.5 = (f32[8,2,1024]{2,1,0:T(2,128)S(1)}, f32[8,2,1024]{2,1,0:T(2,128)S(1)}, u32[]{:S(2)}, u32[]{:S(2)}) collective-permute-start(f32[8,2,1024]{2,1,0:T(2,128)S(1)} %pad_maximum_fusion), channel_id=1, source_target_pairs={{4,20},{24,8},{5,21},{25,9},{6,22},{26,10},{7,23},{27,11}} | collective-permute-start | bytes 196616 | tf_op jit(solution)/shard_map/ppermute | solution.py:304
  39.3 8.1 %collective-permute-start.6 = (f32[8,2,1024]{2,1,0:T(2,128)S(1)}, f32[8,2,1024]{2,1,0:T(2,128)S(1)}, u32[]{:S(2)}, u32[]{:S(2)}) collective-permute-start(f32[8,2,1024]{2,1,0:T(2,128)S(1)} %pad_maximum_fusion), channel_id=1, source_target_pairs={{4,28},{24,0},{5,29},{25,1},{6,30},{26,2},{7,31},{27,3}} | collective-permute-start | bytes 196616 | tf_op jit(solution)/shard_map/ppermute | solution.py:304
  53.2 1.5 copy-start.4
  54.7 8.3 %copy-start.8 = (bf16[1024,896]{1,0:T(8,128)(2,1)S(1)}, bf16[1024,896]{1,0:T(8,128)(2,1)}, u32[]{:S(2)}) copy-start(bf16[1024,896]{1,0:T(8,128)(2,1)} %copy-done.7) | copy-start | bytes 5505028
  54.7 9.6 %copy-start.12 = (f32[2,6]{1,0:T(2,128)S(1)}, f32[2,6]{1,0:T(2,128)}, u32[]{:S(2)}) copy-start(f32[2,6]{1,0:T(2,128)} %param.14) | copy-start | bytes 148
  54.7 15.4 %copy-start.10 = (f32[1,1024]{1,0:T(1,128)S(1)}, f32[1,1024]{1,0:T(1,128)}, u32[]{:S(2)}) copy-start(f32[1,1024]{1,0:T(1,128)} %param.15) | copy-start | bytes 12292
  56.5 61.6 %collective-permute-start.14 = (bf16[1024,896]{1,0:T(8,128)(2,1)S(1)}, bf16[1024,896]{1,0:T(8,128)(2,1)S(1)}, u32[]{:S(2)}, u32[]{:S(2)}) collective-permute-start(bf16[1024,896]{1,0:T(8,128)(2,1)S(1)} %either.1), channel_id=1, source_target_pairs={{12,0},{16,28},{0,16},{28,12},{13,1},{17,29},{1,17},{29,13},{14,2}... | collective-permute-start | bytes 5505032 | tf_op jit(solution)/shard_map/ppermute | solution.py:313
  63.0 82.7 %collective-permute-start.13 = (bf16[1024,896]{1,0:T(8,128)(2,1)S(1)}, bf16[1024,896]{1,0:T(8,128)(2,1)S(1)}, u32[]{:S(2)}, u32[]{:S(2)}) collective-permute-start(bf16[1024,896]{1,0:T(8,128)(2,1)S(1)} %copy-done.8), channel_id=1, source_target_pairs={{4,16},{12,0},{16,28},{24,12},{5,17},{13,1},{17,29},{25,13},{6,18}... | collective-permute-start | bytes 5505032 | tf_op jit(solution)/shard_map/ppermute | solution.py:314
  64.4 84.0 %collective-permute-start.12 = (bf16[1024,640]{1,0:T(8,128)(2,1)S(1)}, bf16[1024,640]{1,0:T(8,128)(2,1)S(1)}, u32[]{:S(2)}, u32[]{:S(2)}) collective-permute-start(bf16[1024,640]{1,0:T(8,128)(2,1)S(1)} %left.7.own_ref), channel_id=1, source_target_pairs={{0,12},{8,20},{12,24},{16,4},{20,8},{28,16},{1,13},{9,21},{13,25},... | collective-permute-start | bytes 3932168 | tf_op jit(solution)/shard_map/ppermute | solution.py:315
  70.2 3.8 %collective-permute-start.7 = (f32[2,1024]{1,0:T(2,128)S(1)}, f32[2,1024]{1,0:T(2,128)S(1)}, u32[]{:S(2)}, u32[]{:S(2)}) collective-permute-start(f32[2,1024]{1,0:T(2,128)S(1)} %get-tuple-element.36), channel_id=1, source_target_pairs={{0,1},{1,2},{2,3},{4,5},{5,6},{6,7},{8,9},{9,10},{10,11},{12,13},{... | collective-permute-start | bytes 24584 | tf_op jit(solution)/shard_map/ppermute | solution.py:30
  71.5 2.5 %copy-start.6 = (bf16[1024,256]{1,0:T(8,128)(2,1)S(1)}, bf16[1024,256]{1,0:T(8,128)(2,1)}, u32[]{:S(2)}) copy-start(bf16[1024,256]{1,0:T(8,128)(2,1)} %copy-done.5) | copy-start | bytes 1572868
  71.5 43.8 %collective-permute-start.8 = (f32[2,1024]{1,0:T(2,128)S(1)}, f32[2,1024]{1,0:T(2,128)S(1)}, u32[]{:S(2)}, u32[]{:S(2)}) collective-permute-start(f32[2,1024]{1,0:T(2,128)S(1)} %get-tuple-element.37), channel_id=1, source_target_pairs={{1,0},{2,1},{3,2},{5,4},{6,5},{7,6},{9,8},{10,9},{11,10},{13,12},{... | collective-permute-start | bytes 24584 | tf_op jit(solution)/shard_map/ppermute | solution.py:30
  74.0 81.5 %collective-permute-start.10 = (bf16[1024,256]{1,0:T(8,128)(2,1)S(1)}, bf16[1024,256]{1,0:T(8,128)(2,1)S(1)}, u32[]{:S(2)}, u32[]{:S(2)}) collective-permute-start(bf16[1024,256]{1,0:T(8,128)(2,1)S(1)} %copy-done.6), channel_id=1, source_target_pairs={{0,12},{8,20},{12,24},{16,4},{20,8},{28,16},{1,13},{9,21},{13,25},... | collective-permute-start | bytes 1572872 | tf_op jit(solution)/shard_map/ppermute | solution.py:319
  115.3 40.2 %collective-permute-start.11 = (bf16[1024,256]{1,0:T(8,128)(2,1)S(1)}, bf16[1024,256]{1,0:T(8,128)(2,1)S(1)}, u32[]{:S(2)}, u32[]{:S(2)}) collective-permute-start(bf16[1024,256]{1,0:T(8,128)(2,1)S(1)} %copy-done.6), channel_id=1, source_target_pairs={{4,16},{12,0},{16,28},{24,12},{5,17},{13,1},{17,29},{25,13},{6,18}... | collective-permute-start | bytes 1572872 | tf_op jit(solution)/shard_map/ppermute | solution.py:318
where the time goes:
time: 161 us; the launch traced here: 158 us
  starting transfers between devices  74.1 us (46%)
  waiting for transfers between devices  38.8 us (24%)
  Pallas kernels  28.8 us (18%)
  local copies, waits for them, and re-layouts  11.2 us (7%)
  between operations  4.35 us (3%)
    ppermute x1, starting transfers between devices, on_device(): first[3] = lax.ppermute(left[3], 'energy', STRAIGHT)  41.3 us
    ppermute x1, waiting for transfers between devices, on_device(): crossed = lax.ppermute(middle, 'energy', CROSS)  22.6 us
    pallas_call x4, Pallas kernels, photon_of(): pl.pallas_call(functools.partial(photon_body, chunk, skips), in_specs=in_...  13.8 us
    pallas_call x5, Pallas kernels, left_of(): pl.pallas_call(functools.partial(left_body, chunk, streamed), in_specs=[p...  11 us
    unnamed x28, local copies, waits for them, and re-layouts  9.95 us
    ppermute x1, starting transfers between devices, on_device(): first[1] = lax.ppermute(left[1], 'energy', STRAIGHT)  6.86 us
    ppermute x3, waiting for transfers between devices, on_device(): held += lax.ppermute(everyone, 'energy', route)  6.73 us
    ppermute x1, starting transfers between devices, on_device(): second[0] = lax.ppermute(onward, 'energy', EDGES + second_hops)  6.45 us
  transfers between devices with their start and end apart: 15, of which 4 were waited for; matrix products, arithmetic and copies ran while one was open for 2% of the time, Pallas kernels for 16%

commit v1 on v0

--- a/solution.py
+++ b/solution.py
@@ -96,6 +96,14 @@
     upward = (offset[None, :, :] == phonon_lags[:, None, None]).astype(jnp.float32)
     downward = (offset[None, :, :] == -phonon_lags[:, None, None]).astype(jnp.float32)
     return jnp.sum(first[:, None, None] * upward + second[:, None, None] * downward, axis=0)
+
+
+def lag_sums(rows, everyone, phonon_lags, strengths):
+    cols = jnp.arange(everyone.shape[0], dtype=jnp.int32)
+    k_less = lag_kernel(rows, cols, phonon_lags, strengths[0], strengths[1])
+    k_great = lag_kernel(rows, cols, phonon_lags, strengths[1], strengths[0])
+    kernels = jnp.stack([k_less, k_great], axis=-1)
+    return jnp.sum(kernels[..., None] * everyone[None], axis=1)
 
 
 def left_body(chunk, streamed, lesser_ref, dipole_ref, left_ref, *scratch):
@@ -183,13 +191,13 @@
     out_ref[...] = block_ref[...]
 
 
-def held_of(block):
+def held_of(block, flops):
     return pl.pallas_call(
         held_body,
         in_specs=[pl.BlockSpec(memory_space=pltpu.VMEM)],
         out_specs=pl.BlockSpec(memory_space=pltpu.VMEM),
         out_shape=jax.ShapeDtypeStruct(block.shape, block.dtype),
-        cost_estimate=pl.CostEstimate(flops=4000000000, bytes_accessed=0, transcendentals=0),
+        cost_estimate=pl.CostEstimate(flops=flops, bytes_accessed=0, transcendentals=0),
         compiler_params=pltpu.CompilerParams(vmem_limit_bytes=VMEM_BYTES),
         name="held",
     )(block)
@@ -299,21 +307,24 @@
             everyone = jnp.concatenate(
                 [jnp.where(is_low, everyone, other), jnp.where(is_low, other, everyone)], axis=0
             )
-        held = jnp.where(any_of(own, [hub for hub, _ in BETWEEN_HUBS]), everyone, 0.0)
-        for route in FROM_HUBS:
-            held += lax.ppermute(everyone, "energy", route)
-        everyone = held
+        hubs = [hub for hub, _ in BETWEEN_HUBS]
+        to = [[own] + [dict(route)[hub] for route in FROM_HUBS] for hub in hubs]
+        rows = [jnp.where(is_low, low, high) for low, high in zip(*to)]
+        sums = lag_sums(jnp.stack(rows), everyone, phonon_lags, phonon_strengths)
+        correlated = jnp.where(any_of(own, hubs), sums[0], 0.0)
+        for n, route in enumerate(FROM_HUBS):
+            correlated += lax.ppermute(sums[n + 1], "energy", route)
 
         middle = left_of(lesser, dipole, MIDDLE)
-        first[0], everyone, *left, middle = lax.optimization_barrier(
-            (first[0], everyone, *left, middle)
+        first[0], correlated, *left, middle = lax.optimization_barrier(
+            (first[0], correlated, *left, middle)
         )
         relays = any_of(own, [by for by, _ in second_hops])
         onward = either_of(relays, first[0], left[0])
         second[0] = lax.ppermute(onward, "energy", EDGES + second_hops)
         crossed = lax.ppermute(middle, "energy", CROSS)
         first[2] = lax.ppermute(left[2], "energy", STRAIGHT)
-        first[1] = held_of(first[1])
+        first[1] = held_of(first[1], 4000000000)
         first[1], left[3] = lax.optimization_barrier((first[1], left[3]))
         second[3] = lax.ppermute(left[3], "energy", CROSS)
         first[3] = lax.ppermute(left[3], "energy", STRAIGHT)
@@ -326,6 +337,7 @@
         while step < count:
             everyone = doubled(everyone, "energy", step)
             step *= 2
+        correlated = lag_sums(own[None], everyone, phonon_lags, phonon_strengths)[0]
         first = [shifted(block, "energy", PHOT_BLOCKS) for block in left]
         second = [shifted(block, "energy", -PHOT_BLOCKS) for block in left]
         weights = [weight_low, weight_high]
@@ -340,13 +352,7 @@
     else:
         sides = [[(low, 0), (high, 0)] for low, high in zip(first, second)]
 
-    own_rows = own * e_count + jnp.arange(e_count, dtype=jnp.int32)
-    all_rows = jnp.arange(e_count * count, dtype=jnp.int32)
-    k_less = lag_kernel(own_rows, all_rows, phonon_lags, phonon_strengths[0], phonon_strengths[1])
-    k_great = lag_kernel(own_rows, all_rows, phonon_lags, phonon_strengths[1], phonon_strengths[0])
-    corr_less = jnp.sum(k_less[0][:, None] * everyone[:, 0], axis=0)
-    corr_great = jnp.sum(k_great[0][:, None] * everyone[:, 1], axis=0)
-    correlated = jnp.stack([corr_less, corr_great])
+    correlated = held_of(correlated, 7000000000)
     below = shifted(slab_coupling * correlated, "slab", 1)
     above = shifted(correlated, "slab", -1)
     phon_less, phon_great = correlated + below + slab_coupling * above

time: 161 us -> 159 us (0.988)
  starting transfers between devices: 74.1 us -> 68.5 us
  Pallas kernels: 28.8 us -> 33.2 us
    ppermute x1, waiting for transfers between devices: 5.78 us -> 14.5 us  [on_device(): first[0] = lax.ppermute(left[0], 'energy', STRAIGHT + hops)]
    ppermute x1, starting transfers between devices: 41.3 us -> 32.7 us  [on_device(): first[3] = lax.ppermute(left[3], 'energy', STRAIGHT)]
    ppermute x3, waiting for transfers between devices: 6.73 us -> 0.01 us  [on_device(): correlated += lax.ppermute(sums[n + 1], 'energy', route)]
    pallas_call x4, Pallas kernels: 13.8 us -> 15.9 us  [photon_of(): pl.pallas_call(functools.partial(photon_body, chunk, skips), in_specs=in_...]
    ppermute x2, starting transfers between devices: 2.71 us -> 4.45 us  [shifted(): lax.ppermute(block, axis, [(i - distance, i) for i in devices if i - dist...]
    unnamed x28 -> x26, local copies, waits for them, and re-layouts: 9.95 us -> 8.75 us
  transfers between devices with their start and end apart: 15 -> 15, of which waited for: 4 -> 3; matrix products, arithmetic and copies ran while one was open for 2% -> 2% of each run, Pallas kernels for 16% -> 19%
where the time goes in v1:
time: 159 us; the launch traced here: 157 us
  starting transfers between devices  68.5 us (43%)
  waiting for transfers between devices  40.1 us (25%)
  Pallas kernels  33.2 us (21%)
  local copies, waits for them, and re-layouts  10 us (6%)
  between operations  4.34 us (3%)
    ppermute x1, starting transfers between devices, on_device(): first[3] = lax.ppermute(left[3], 'energy', STRAIGHT)  32.7 us
    ppermute x1, waiting for transfers between devices, on_device(): crossed = lax.ppermute(middle, 'energy', CROSS)  23.5 us
    pallas_call x4, Pallas kernels, photon_of(): pl.pallas_call(functools.partial(photon_body, chunk, skips), in_specs=in_...  15.9 us
    ppermute x1, waiting for transfers between devices, on_device(): first[0] = lax.ppermute(left[0], 'energy', STRAIGHT + hops)  14.5 us
    pallas_call x5, Pallas kernels, left_of(): pl.pallas_call(functools.partial(left_body, chunk, streamed), in_specs=[p...  12.3 us
    unnamed x26, local copies, waits for them, and re-layouts  8.75 us
    ppermute x1, starting transfers between devices, on_device(): first[1] = lax.ppermute(left[1], 'energy', STRAIGHT)  8.18 us
    ppermute x1, starting transfers between devices, on_device(): second[0] = lax.ppermute(onward, 'energy', EDGES + second_hops)  6.34 us
  transfers between devices with their start and end apart: 15, of which 3 were waited for; matrix products, arithmetic and copies ran while one was open for 2% of the time, Pallas kernels for 19%

profile of v1, /device:TPU:0, one launch (start us, length us, event | category | flops | bytes accessed | tf_op | source)
XLA Modules:
  0.0 157.4 jit_solution(15245524722295213784)
XLA Ops:
  0.6 0.0 copy-start
  0.6 0.8 copy-done.8
  1.5 1.0 diagonals.1
  2.5 3.0 %collective-permute-start = (f32[1,2,1024]{2,1,0:T(2,128)S(1)}, f32[1,2,1024]{2,1,0:T(2,128)S(1)}, u32[]{:S(2)}, u32[]{:S(2)}) collective-permute-start(f32[1,2,1024]{2,1,0:T(2,128)S(1)} %diagonals.1), channel_id=1, source_target_pairs={{0,4},{4,0},{8,12},{12,8},{16,20},{20,16},{24,28},{28,24},{1,5},{5... | collective-permute-start | bytes 24584 | tf_op jit(solution)/shard_map/ppermute | solution.py:46
  5.6 0.0 copy-done
  5.6 4.1 %left.5.no_ref.own_ref = bf16[1024,896]{1,0:T(8,128)(2,1)S(1)} custom-call(bf16[1,1,2,1024,1024]{4,3,2,1,0:T(8,128)(2,1)} %lesser_ref.11, bf16[1,1024,1024]{2,1,0:T(8,128)(2,1)S(1)} %copy-done), custom_call_target="tpu_custom_call" | custom-call | tf_op jit(solution)/shard_map/left/pallas_call | solution.py:145
  9.6 0.0 copy-start.3
  9.6 1.2 copy-done.3
  10.9 0.0 collective-permute-done
  10.9 1.6 collective-permute-start.1
  12.5 0.0 copy-done.11
  12.5 0.1 pad_add_fusion
  12.6 0.1 iota_subtract_fusion
  12.7 0.7 collective-permute-start.2
  13.3 0.1 fusion.1
  13.4 0.0 collective-permute-done.2
  13.5 0.7 collective-permute-start.3
  14.2 0.0 collective-permute-done.3
  14.3 0.2 multiply_reduce_fusion
  14.5 0.7 collective-permute-start.4
  15.1 0.7 collective-permute-start.5
  15.8 1.3 collective-permute-start.6
  17.1 0.0 copy-start.1
  17.1 2.2 %copy-done.1 = bf16[1,1,2,1024,1024]{4,3,2,1,0:T(8,128)(2,1)S(1)} copy-done((bf16[1,1,2,1024,1024]{4,3,2,1,0:T(8,128)(2,1)S(1)}, bf16[1,1,2,1024,1024]{4,3,2,1,0:T(8,128)(2,1)}, u32[]{:S(2)}) %copy-start.1) | copy-done | bytes 4194328
  19.3 1.6 left.6.own_ref
  20.8 8.2 %collective-permute-start.9 = (bf16[1024,256]{1,0:T(8,128)(2,1)}, bf16[1024,256]{1,0:T(8,128)(2,1)}, u32[]{:S(2)}, u32[]{:S(2)}) collective-permute-start(bf16[1024,256]{1,0:T(8,128)(2,1)} %left.6.own_ref), channel_id=1, source_target_pairs={{0,12},{8,20},{12,24},{16,4},{20,8},{28,16},{1,13},{9,21},{13,25},... | collective-permute-start | bytes 1572872 | tf_op jit(solution)/shard_map/ppermute | solution.py:302
  29.0 2.2 %copy-done.2 = bf16[1,1,2,1024,1024]{4,3,2,1,0:T(8,128)(2,1)S(1)} copy-done((bf16[1,1,2,1024,1024]{4,3,2,1,0:T(8,128)(2,1)S(1)}, bf16[1,1,2,1024,1024]{4,3,2,1,0:T(8,128)(2,1)}, u32[]{:S(2)}) %copy-start.2) | copy-done | bytes 4194328
  31.2 3.6 %left.9 = bf16[1024,896]{1,0:T(8,128)(2,1)} custom-call(bf16[1,1,2,1024,1024]{4,3,2,1,0:T(8,128)(2,1)S(1)} %copy-done.2, bf16[1,1024,1024]{2,1,0:T(8,128)(2,1)S(1)} %copy-done), custom_call_target="tpu_custom_call" | custom-call | tf_op jit(solution)/shard_map/left/pallas_call | solution.py:145
  34.8 1.8 %left.7.own_ref = bf16[1024,640]{1,0:T(8,128)(2,1)S(1)} custom-call(bf16[1,1,2,1024,1024]{4,3,2,1,0:T(8,128)(2,1)S(1)} %copy-done.2, bf16[1,1024,1024]{2,1,0:T(8,128)(2,1)S(1)} %copy-done), custom_call_target="tpu_custom_call" | custom-call | tf_op jit(solution)/shard_map/left/pallas_call | solution.py:145
  36.6 1.2 left.8.own_ref
  37.9 0.8 copy-done.6
  38.7 0.0 collective-permute-done.4
  38.7 0.0 collective-permute-done.5
  38.7 0.0 collective-permute-done.6
  38.7 14.5 %collective-permute-done.1.yes_ref.rest_0_ = bf16[1024,896]{1,0:T(8,128)(2,1)} collective-permute-done((bf16[1024,896]{1,0:T(8,128)(2,1)}, bf16[1024,896]{1,0:T(8,128)(2,1)}, u32[]{:S(2)}, u32[]{:S(2)}) %collective-permute-start.1) | collective-permute-done | bytes 1835040 | tf_op jit(solution)/shard_map/ppermute | solution.py:301
  53.2 1.5 copy-done.4
  54.7 2.9 %either.1 = bf16[1024,896]{1,0:T(8,128)(2,1)} custom-call(s32[1]{0:T(128)} %bitcast.18.flag_ref, bf16[1024,896]{1,0:T(8,128)(2,1)} %collective-permute-done.1.yes_ref.rest_0_, bf16[1024,896]{1,0:T(8,128)(2,1)S(1)} %copy-done.4), custom_call_target="tpu_custom_call" | custom-call | tf_op jit(solution)/shard_map/either/pallas_call | solution.py:176
  57.7 6.3 %collective-permute-start.14 = (bf16[1024,896]{1,0:T(8,128)(2,1)}, bf16[1024,896]{1,0:T(8,128)(2,1)}, u32[]{:S(2)}, u32[]{:S(2)}) collective-permute-start(bf16[1024,896]{1,0:T(8,128)(2,1)} %either.1), channel_id=1, source_target_pairs={{12,0},{16,28},{0,16},{28,12},{13,1},{17,29},{1,17},{29,13},{14,2}... | collective-permute-start | bytes 5505032 | tf_op jit(solution)/shard_map/ppermute | solution.py:324
  64.0 1.3 collective-permute-start.13
  65.3 0.6 fusion.8
  69.1 0.0 copy-start.9
  69.1 5.5 %collective-permute-start.12 = (bf16[1024,640]{1,0:T(8,128)(2,1)S(1)}, bf16[1024,640]{1,0:T(8,128)(2,1)S(1)}, u32[]{:S(2)}, u32[]{:S(2)}) collective-permute-start(bf16[1024,640]{1,0:T(8,128)(2,1)S(1)} %left.7.own_ref), channel_id=1, source_target_pairs={{0,12},{8,20},{12,24},{16,4},{20,8},{28,16},{1,13},{9,21},{13,25},... | collective-permute-start | bytes 3932168 | tf_op jit(solution)/shard_map/ppermute | solution.py:326
  74.6 1.3 collective-permute-start.8
  75.9 0.0 copy-done.9
  76.0 0.0 copy-start.5
  76.0 0.0 collective-permute-done.9.block_ref
  76.0 3.2 %collective-permute-start.7 = (f32[2,1024]{1,0:T(2,128)S(1)}, f32[2,1024]{1,0:T(2,128)S(1)}, u32[]{:S(2)}, u32[]{:S(2)}) collective-permute-start(f32[2,1024]{1,0:T(2,128)S(1)} %broadcast_multiply_fusion), channel_id=1, source_target_pairs={{0,1},{1,2},{2,3},{4,5},{5,6},{6,7},{8,9},{9,10},{10,11},{12,13},{... | collective-permute-start | bytes 24584 | tf_op jit(solution)/shard_map/ppermute | solution.py:30
  79.2 1.1 held.3.rest_0_
  80.3 0.0 collective-permute-done.7
  80.3 0.0 copy-done.7
  80.3 32.7 %collective-permute-start.10 = (bf16[1024,256]{1,0:T(8,128)(2,1)S(1)}, bf16[1024,256]{1,0:T(8,128)(2,1)S(1)}, u32[]{:S(2)}, u32[]{:S(2)}) collective-permute-start(bf16[1024,256]{1,0:T(8,128)(2,1)S(1)} %copy-done.7), channel_id=1, source_target_pairs={{0,12},{8,20},{12,24},{16,4},{20,8},{28,16},{1,13},{9,21},{13,25},... | collective-permute-start | bytes 1572872 | tf_op jit(solution)/shard_map/ppermute | solution.py:330
  113.0 0.0 collective-permute-done.8
  113.0 1.5 collective-permute-start.11
  114.5 0.6 pad_maximum_fusion.4.factors_ref
  115.1 0.6 slice_bitcast_fusion.3
  115.7 0.0 collective-permute-done.14.rest_1_
  115.8 5.5 %photon.4.rest_2_ = bf16[1,1,2,1024,1024]{4,3,2,1,0:T(8,128)(2,1)} custom-call(f32[4]{0:T(128)S(1)} %pad_maximum_fusion.4.factors_ref, bf16[1,1024,1024]{2,1,0:T(8,128)(2,1)S(1)} %copy-done, f32[1,1024]{1,0:T(1,128)S(1)} %get-tuple-element.36.phonon_ref, bf16[1024,896]{1,0:T(8,128)(2,1)S(1)} %copy-done.5, ...), custom_call_target="tpu_custom_call" | custom-call | tf_op jit(solution)/shard_map/photon/pallas_call | solution.py:262
  121.3 23.5 %collective-permute-done.13.rest_1_ = bf16[1024,896]{1,0:T(8,128)(2,1)} collective-permute-done((bf16[1024,896]{1,0:T(8,128)(2,1)}, bf16[1024,896]{1,0:T(8,128)(2,1)}, u32[]{:S(2)}, u32[]{:S(2)}) %collective-permute-start.13) | collective-permute-done | bytes 1835040 | tf_op jit(solution)/shard_map/ppermute | solution.py:325
  144.7 3.4 %photon.5.rest_2_ = bf16[1,1,2,1024,1024]{4,3,2,1,0:T(8,128)(2,1)} custom-call(f32[4]{0:T(128)S(1)} %pad_maximum_fusion.4.factors_ref, bf16[1,1024,1024]{2,1,0:T(8,128)(2,1)S(1)} %copy-done, f32[1,1024]{1,0:T(1,128)S(1)} %get-tuple-element.36.phonon_ref, bf16[1024,256]{1,0:T(8,128)(2,1)} %left.6.own_ref, ...), custom_call_target="tpu_custom_call", output_to_operand_aliasing={{}: (6, {})} | custom-call | tf_op jit(solution)/shard_map/photon/pallas_call | solution.py:262
  148.1 0.0 collective-permute-done.12.rest_0_
  148.1 4.4 %photon.6.rest_2_ = bf16[1,1,2,1024,1024]{4,3,2,1,0:T(8,128)(2,1)} custom-call(f32[4]{0:T(128)S(1)} %pad_maximum_fusion.4.factors_ref, bf16[1,1024,1024]{2,1,0:T(8,128)(2,1)S(1)} %copy-done, f32[1,1024]{1,0:T(1,128)S(1)} %get-tuple-element.36.phonon_ref, bf16[1024,640]{1,0:T(8,128)(2,1)S(1)} %left.7.own_ref, ...), custom_call_target="tpu_custom_call", output_to_operand_aliasing={{}: (6, {})} | custom-call | tf_op jit(solution)/shard_map/photon/pallas_call | solution.py:262
  152.5 2.1 %collective-permute-done.10.rest_0_ = bf16[1024,256]{1,0:T(8,128)(2,1)S(1)} collective-permute-done((bf16[1024,256]{1,0:T(8,128)(2,1)S(1)}, bf16[1024,256]{1,0:T(8,128)(2,1)S(1)}, u32[]{:S(2)}, u32[]{:S(2)}) %collective-permute-start.10) | collective-permute-done | bytes 524320 | tf_op jit(solution)/shard_map/ppermute | solution.py:330
  154.6 0.0 collective-permute-done.11.rest_1_
  154.6 2.6 %photon.7 = bf16[1,1,2,1024,1024]{4,3,2,1,0:T(8,128)(2,1)} custom-call(f32[4]{0:T(128)S(1)} %pad_maximum_fusion.4.factors_ref, bf16[1,1024,1024]{2,1,0:T(8,128)(2,1)S(1)} %copy-done, f32[1,1024]{1,0:T(1,128)S(1)} %get-tuple-element.36.phonon_ref, bf16[1024,256]{1,0:T(8,128)(2,1)S(1)} %copy-done.7, ...), custom_call_target="tpu_custom_call", output_to_operand_aliasing={{}: (6, {})} | custom-call | tf_op jit(solution)/shard_map/photon/pallas_call | solution.py:262
  (27 shorter events, 0.2 us)
Async XLA Ops:
  0.6 4.9 %copy-start = (bf16[1,1024,1024]{2,1,0:T(8,128)(2,1)S(1)}, bf16[1,1024,1024]{2,1,0:T(8,128)(2,1)}, u32[]{:S(2)}) copy-start(bf16[1,1024,1024]{2,1,0:T(8,128)(2,1)} %dipole_ref.17) | copy-start | bytes 6291460
  0.6 0.8 copy-start.8
  2.5 8.3 %collective-permute-start = (f32[1,2,1024]{2,1,0:T(2,128)S(1)}, f32[1,2,1024]{2,1,0:T(2,128)S(1)}, u32[]{:S(2)}, u32[]{:S(2)}) collective-permute-start(f32[1,2,1024]{2,1,0:T(2,128)S(1)} %diagonals.1), channel_id=1, source_target_pairs={{0,4},{4,0},{8,12},{12,8},{16,20},{20,16},{24,28},{28,24},{1,5},{5... | collective-permute-start | bytes 24584 | tf_op jit(solution)/shard_map/ppermute | solution.py:46
  5.6 6.9 %copy-start.11 = (f32[2,6]{1,0:T(2,128)S(1)}, f32[2,6]{1,0:T(2,128)}, u32[]{:S(2)}) copy-start(f32[2,6]{1,0:T(2,128)} %param.14) | copy-start | bytes 148
  5.6 6.9 %copy-start.12 = (s32[6]{0:T(128)S(1)}, s32[6]{0:T(128)}, u32[]{:S(2)}) copy-start(s32[6]{0:T(128)} %param.13) | copy-start | bytes 76
  9.6 1.2 copy-start.3
  10.9 42.3 %collective-permute-start.1 = (bf16[1024,896]{1,0:T(8,128)(2,1)}, bf16[1024,896]{1,0:T(8,128)(2,1)}, u32[]{:S(2)}, u32[]{:S(2)}) collective-permute-start(bf16[1024,896]{1,0:T(8,128)(2,1)} %copy-done.3), channel_id=1, source_target_pairs={{0,12},{8,20},{12,24},{16,4},{20,8},{28,16},{4,0},{24,28},{1,13},{... | collective-permute-start | bytes 5505032 | tf_op jit(solution)/shard_map/ppermute | solution.py:301
  12.7 0.8 collective-permute-start.2
  13.5 0.7 collective-permute-start.3
  14.5 24.2 %collective-permute-start.4 = (f32[2,1024]{1,0:T(2,128)S(1)}, f32[2,1024]{1,0:T(2,128)S(1)}, u32[]{:S(2)}, u32[]{:S(2)}) collective-permute-start(f32[2,1024]{1,0:T(2,128)S(1)} %get-tuple-element.28), channel_id=1, source_target_pairs={{4,12},{24,16},{5,13},{25,17},{6,14},{26,18},{7,15},{27,19}} | collective-permute-start | bytes 24584 | tf_op jit(solution)/shard_map/ppermute | solution.py:316
  15.1 23.6 %collective-permute-start.5 = (f32[2,1024]{1,0:T(2,128)S(1)}, f32[2,1024]{1,0:T(2,128)S(1)}, u32[]{:S(2)}, u32[]{:S(2)}) collective-permute-start(f32[2,1024]{1,0:T(2,128)S(1)} %get-tuple-element.30), channel_id=1, source_target_pairs={{4,20},{24,8},{5,21},{25,9},{6,22},{26,10},{7,23},{27,11}} | collective-permute-start | bytes 24584 | tf_op jit(solution)/shard_map/ppermute | solution.py:316
  15.8 22.9 %collective-permute-start.6 = (f32[2,1024]{1,0:T(2,128)S(1)}, f32[2,1024]{1,0:T(2,128)S(1)}, u32[]{:S(2)}, u32[]{:S(2)}) collective-permute-start(f32[2,1024]{1,0:T(2,128)S(1)} %get-tuple-element.29), channel_id=1, source_target_pairs={{4,28},{24,0},{5,29},{25,1},{6,30},{26,2},{7,31},{27,3}} | collective-permute-start | bytes 24584 | tf_op jit(solution)/shard_map/ppermute | solution.py:316
  17.1 2.2 %copy-start.1 = (bf16[1,1,2,1024,1024]{4,3,2,1,0:T(8,128)(2,1)S(1)}, bf16[1,1,2,1024,1024]{4,3,2,1,0:T(8,128)(2,1)}, u32[]{:S(2)}) copy-start(bf16[1,1,2,1024,1024]{4,3,2,1,0:T(8,128)(2,1)} %lesser_ref.11) | copy-start | bytes 12582916
  20.8 55.2 %collective-permute-start.9 = (bf16[1024,256]{1,0:T(8,128)(2,1)}, bf16[1024,256]{1,0:T(8,128)(2,1)}, u32[]{:S(2)}, u32[]{:S(2)}) collective-permute-start(bf16[1024,256]{1,0:T(8,128)(2,1)} %left.6.own_ref), channel_id=1, source_target_pairs={{0,12},{8,20},{12,24},{16,4},{20,8},{28,16},{1,13},{9,21},{13,25},... | collective-permute-start | bytes 1572872 | tf_op jit(solution)/shard_map/ppermute | solution.py:302
  29.0 2.2 %copy-start.2 = (bf16[1,1,2,1024,1024]{4,3,2,1,0:T(8,128)(2,1)S(1)}, bf16[1,1,2,1024,1024]{4,3,2,1,0:T(8,128)(2,1)}, u32[]{:S(2)}) copy-start(bf16[1,1,2,1024,1024]{4,3,2,1,0:T(8,128)(2,1)} %lesser_ref.11) | copy-start | bytes 12582916
  37.9 0.8 copy-start.6
  53.2 1.5 copy-start.4
  54.7 10.6 %copy-start.10 = (f32[1,3]{1,0:T(1,128)S(1)}, f32[1,3]{1,0:T(1,128)}, u32[]{:S(2)}) copy-start(f32[1,3]{1,0:T(1,128)} %param.11) | copy-start | bytes 40
  57.7 58.1 %collective-permute-start.14 = (bf16[1024,896]{1,0:T(8,128)(2,1)}, bf16[1024,896]{1,0:T(8,128)(2,1)}, u32[]{:S(2)}, u32[]{:S(2)}) collective-permute-start(bf16[1024,896]{1,0:T(8,128)(2,1)} %either.1), channel_id=1, source_target_pairs={{12,0},{16,28},{0,16},{28,12},{13,1},{17,29},{1,17},{29,13},{14,2}... | collective-permute-start | bytes 5505032 | tf_op jit(solution)/shard_map/ppermute | solution.py:324
  64.0 80.7 %collective-permute-start.13 = (bf16[1024,896]{1,0:T(8,128)(2,1)}, bf16[1024,896]{1,0:T(8,128)(2,1)}, u32[]{:S(2)}, u32[]{:S(2)}) collective-permute-start(bf16[1024,896]{1,0:T(8,128)(2,1)} %left.9), channel_id=1, source_target_pairs={{4,16},{12,0},{16,28},{24,12},{5,17},{13,1},{17,29},{25,13},{6,18}... | collective-permute-start | bytes 5505032 | tf_op jit(solution)/shard_map/ppermute | solution.py:325
  69.1 6.9 %copy-start.9 = (f32[1,1024]{1,0:T(1,128)S(1)}, f32[1,1024]{1,0:T(1,128)}, u32[]{:S(2)}) copy-start(f32[1,1024]{1,0:T(1,128)} %param.15) | copy-start | bytes 12292
  69.1 79.0 %collective-permute-start.12 = (bf16[1024,640]{1,0:T(8,128)(2,1)S(1)}, bf16[1024,640]{1,0:T(8,128)(2,1)S(1)}, u32[]{:S(2)}, u32[]{:S(2)}) collective-permute-start(bf16[1024,640]{1,0:T(8,128)(2,1)S(1)} %left.7.own_ref), channel_id=1, source_target_pairs={{0,12},{8,20},{12,24},{16,4},{20,8},{28,16},{1,13},{9,21},{13,25},... | collective-permute-start | bytes 3932168 | tf_op jit(solution)/shard_map/ppermute | solution.py:326
  74.6 38.4 %collective-permute-start.8 = (f32[2,1024]{1,0:T(2,128)S(1)}, f32[2,1024]{1,0:T(2,128)S(1)}, u32[]{:S(2)}, u32[]{:S(2)}) collective-permute-start(f32[2,1024]{1,0:T(2,128)S(1)} %held.2), channel_id=1, source_target_pairs={{1,0},{2,1},{3,2},{5,4},{6,5},{7,6},{9,8},{10,9},{11,10},{13,12},{... | collective-permute-start | bytes 24584 | tf_op jit(solution)/shard_map/ppermute | solution.py:30
  76.0 4.3 %copy-start.7 = (bf16[1024,256]{1,0:T(8,128)(2,1)S(1)}, bf16[1024,256]{1,0:T(8,128)(2,1)}, u32[]{:S(2)}) copy-start(bf16[1024,256]{1,0:T(8,128)(2,1)} %copy-done.6) | copy-start | bytes 1572868
  76.0 39.8 %copy-start.5 = (bf16[1024,896]{1,0:T(8,128)(2,1)S(1)}, bf16[1024,896]{1,0:T(8,128)(2,1)}, u32[]{:S(2)}) copy-start(bf16[1024,896]{1,0:T(8,128)(2,1)} %copy-done.3) | copy-start | bytes 5505028
  76.0 4.3 %collective-permute-start.7 = (f32[2,1024]{1,0:T(2,128)S(1)}, f32[2,1024]{1,0:T(2,128)S(1)}, u32[]{:S(2)}, u32[]{:S(2)}) collective-permute-start(f32[2,1024]{1,0:T(2,128)S(1)} %broadcast_multiply_fusion), channel_id=1, source_target_pairs={{0,1},{1,2},{2,3},{4,5},{5,6},{6,7},{8,9},{9,10},{10,11},{12,13},{... | collective-permute-start | bytes 24584 | tf_op jit(solution)/shard_map/ppermute | solution.py:30
  80.3 74.3 %collective-permute-start.10 = (bf16[1024,256]{1,0:T(8,128)(2,1)S(1)}, bf16[1024,256]{1,0:T(8,128)(2,1)S(1)}, u32[]{:S(2)}, u32[]{:S(2)}) collective-permute-start(bf16[1024,256]{1,0:T(8,128)(2,1)S(1)} %copy-done.7), channel_id=1, source_target_pairs={{0,12},{8,20},{12,24},{16,4},{20,8},{28,16},{1,13},{9,21},{13,25},... | collective-permute-start | bytes 1572872 | tf_op jit(solution)/shard_map/ppermute | solution.py:330
  113.0 41.6 %collective-permute-start.11 = (bf16[1024,256]{1,0:T(8,128)(2,1)S(1)}, bf16[1024,256]{1,0:T(8,128)(2,1)S(1)}, u32[]{:S(2)}, u32[]{:S(2)}) collective-permute-start(bf16[1024,256]{1,0:T(8,128)(2,1)S(1)} %copy-done.7), channel_id=1, source_target_pairs={{4,16},{12,0},{16,28},{24,12},{5,17},{13,1},{17,29},{25,13},{6,18}... | collective-permute-start | bytes 1572872 | tf_op jit(solution)/shard_map/ppermute | solution.py:329

commit v2 on v1

--- a/solution.py
+++ b/solution.py
@@ -11,7 +11,8 @@
 CHUNKS = (((0, 0, 7),), ((1, 0, 2),), ((1, 2, 5),), ((1, 7, 1), (0, 7, 1)))
 MIDDLE = ((1, 0, 7),)
 EIGHTHS = 8
-VMEM_BYTES = 20 * 1024 * 1024
+VMEM_BYTES = 14 * 1024 * 1024
+SMALL_VMEM_BYTES = 8 * 1024 * 1024
 EARLY_VMEM_BYTES = 53 * 1024 * 1024
 FIRST_VMEM_BYTES = 48 * 1024 * 1024
 
@@ -152,7 +153,7 @@
         out_shape=jax.ShapeDtypeStruct((width, cols), lesser.dtype),
         scratch_shapes=scratch if streamed else [],
         compiler_params=pltpu.CompilerParams(
-            vmem_limit_bytes=FIRST_VMEM_BYTES if streamed else VMEM_BYTES
+            vmem_limit_bytes=FIRST_VMEM_BYTES if streamed else SMALL_VMEM_BYTES
         ),
         name="left",
     )(lesser, dipole)
@@ -182,7 +183,7 @@
         ],
         out_specs=pl.BlockSpec(memory_space=pltpu.VMEM),
         out_shape=jax.ShapeDtypeStruct(yes.shape, yes.dtype),
-        compiler_params=pltpu.CompilerParams(vmem_limit_bytes=VMEM_BYTES),
+        compiler_params=pltpu.CompilerParams(vmem_limit_bytes=SMALL_VMEM_BYTES),
         name="either",
     )(flag.astype(jnp.int32).reshape(1), yes, no)
 
@@ -198,7 +199,7 @@
         out_specs=pl.BlockSpec(memory_space=pltpu.VMEM),
         out_shape=jax.ShapeDtypeStruct(block.shape, block.dtype),
         cost_estimate=pl.CostEstimate(flops=flops, bytes_accessed=0, transcendentals=0),
-        compiler_params=pltpu.CompilerParams(vmem_limit_bytes=VMEM_BYTES),
+        compiler_params=pltpu.CompilerParams(vmem_limit_bytes=SMALL_VMEM_BYTES),
         name="held",
     )(block)
 
@@ -284,7 +285,6 @@
     phonon_strengths,
     slab_coupling,
 ):
-    e_count = lesser.shape[0]
     width = lesser.shape[-1]
     count = lax.axis_size("energy")
     own = lax.axis_index("energy")

time: 159 us -> 159 us (level)
  no operation moved by 1% of the time
where the time goes in v2:
time: 159 us; the launch traced here: 157 us
  starting transfers between devices  68.5 us (43%)
  waiting for transfers between devices  40.1 us (25%)
  Pallas kernels  33.2 us (21%)
  local copies, waits for them, and re-layouts  10 us (6%)
  between operations  4.34 us (3%)
    ppermute x1, starting transfers between devices, on_device(): first[3] = lax.ppermute(left[3], 'energy', STRAIGHT)  32.7 us
    ppermute x1, waiting for transfers between devices, on_device(): crossed = lax.ppermute(middle, 'energy', CROSS)  23.5 us
    pallas_call x4, Pallas kernels, photon_of(): pl.pallas_call(functools.partial(photon_body, chunk, skips), in_specs=in_...  15.9 us
    ppermute x1, waiting for transfers between devices, on_device(): first[0] = lax.ppermute(left[0], 'energy', STRAIGHT + hops)  14.5 us
    pallas_call x5, Pallas kernels, left_of(): pl.pallas_call(functools.partial(left_body, chunk, streamed), in_specs=[p...  12.3 us
    unnamed x26, local copies, waits for them, and re-layouts  8.75 us
    ppermute x1, starting transfers between devices, on_device(): first[1] = lax.ppermute(left[1], 'energy', STRAIGHT)  8.18 us
    ppermute x1, starting transfers between devices, on_device(): second[0] = lax.ppermute(onward, 'energy', EDGES + second_hops)  6.34 us
  transfers between devices with their start and end apart: 15, of which 3 were waited for; matrix products, arithmetic and copies ran while one was open for 2% of the time, Pallas kernels for 19%

profile of v2, /device:TPU:0, one launch (start us, length us, event | category | flops | bytes accessed | tf_op | source)
XLA Modules:
  0.0 157.4 jit_solution(7488616325565829242)
XLA Ops:
  0.6 0.0 copy-start
  0.6 0.8 copy-done.8
  1.5 1.0 diagonals.1
  2.5 3.0 %collective-permute-start = (f32[1,2,1024]{2,1,0:T(2,128)S(1)}, f32[1,2,1024]{2,1,0:T(2,128)S(1)}, u32[]{:S(2)}, u32[]{:S(2)}) collective-permute-start(f32[1,2,1024]{2,1,0:T(2,128)S(1)} %diagonals.1), channel_id=1, source_target_pairs={{0,4},{4,0},{8,12},{12,8},{16,20},{20,16},{24,28},{28,24},{1,5},{5... | collective-permute-start | bytes 24584 | tf_op jit(solution)/shard_map/ppermute | solution.py:47
  5.6 0.0 copy-done
  5.6 4.1 %left.5.no_ref.own_ref = bf16[1024,896]{1,0:T(8,128)(2,1)S(1)} custom-call(bf16[1,1,2,1024,1024]{4,3,2,1,0:T(8,128)(2,1)} %lesser_ref.11, bf16[1,1024,1024]{2,1,0:T(8,128)(2,1)S(1)} %copy-done), custom_call_target="tpu_custom_call" | custom-call | tf_op jit(solution)/shard_map/left/pallas_call | solution.py:146
  9.6 0.0 copy-start.3
  9.6 1.2 copy-done.3
  10.9 0.0 collective-permute-done
  10.9 1.6 collective-permute-start.1
  12.5 0.0 copy-done.11
  12.5 0.1 pad_add_fusion
  12.6 0.1 iota_subtract_fusion
  12.7 0.7 collective-permute-start.2
  13.3 0.1 fusion.1
  13.4 0.0 collective-permute-done.2
  13.5 0.7 collective-permute-start.3
  14.2 0.0 collective-permute-done.3
  14.3 0.2 multiply_reduce_fusion
  14.5 0.7 collective-permute-start.4
  15.1 0.7 collective-permute-start.5
  15.8 1.3 collective-permute-start.6
  17.1 0.0 copy-start.1
  17.1 2.2 %copy-done.1 = bf16[1,1,2,1024,1024]{4,3,2,1,0:T(8,128)(2,1)S(1)} copy-done((bf16[1,1,2,1024,1024]{4,3,2,1,0:T(8,128)(2,1)S(1)}, bf16[1,1,2,1024,1024]{4,3,2,1,0:T(8,128)(2,1)}, u32[]{:S(2)}) %copy-start.1) | copy-done | bytes 4194328
  19.3 1.6 left.6.own_ref
  20.8 8.2 %collective-permute-start.9 = (bf16[1024,256]{1,0:T(8,128)(2,1)}, bf16[1024,256]{1,0:T(8,128)(2,1)}, u32[]{:S(2)}, u32[]{:S(2)}) collective-permute-start(bf16[1024,256]{1,0:T(8,128)(2,1)} %left.6.own_ref), channel_id=1, source_target_pairs={{0,12},{8,20},{12,24},{16,4},{20,8},{28,16},{1,13},{9,21},{13,25},... | collective-permute-start | bytes 1572872 | tf_op jit(solution)/shard_map/ppermute | solution.py:302
  29.0 2.2 %copy-done.2 = bf16[1,1,2,1024,1024]{4,3,2,1,0:T(8,128)(2,1)S(1)} copy-done((bf16[1,1,2,1024,1024]{4,3,2,1,0:T(8,128)(2,1)S(1)}, bf16[1,1,2,1024,1024]{4,3,2,1,0:T(8,128)(2,1)}, u32[]{:S(2)}) %copy-start.2) | copy-done | bytes 4194328
  31.2 3.6 %left.9 = bf16[1024,896]{1,0:T(8,128)(2,1)} custom-call(bf16[1,1,2,1024,1024]{4,3,2,1,0:T(8,128)(2,1)S(1)} %copy-done.2, bf16[1,1024,1024]{2,1,0:T(8,128)(2,1)S(1)} %copy-done), custom_call_target="tpu_custom_call" | custom-call | tf_op jit(solution)/shard_map/left/pallas_call | solution.py:146
  34.8 1.8 %left.7.own_ref = bf16[1024,640]{1,0:T(8,128)(2,1)S(1)} custom-call(bf16[1,1,2,1024,1024]{4,3,2,1,0:T(8,128)(2,1)S(1)} %copy-done.2, bf16[1,1024,1024]{2,1,0:T(8,128)(2,1)S(1)} %copy-done), custom_call_target="tpu_custom_call" | custom-call | tf_op jit(solution)/shard_map/left/pallas_call | solution.py:146
  36.6 1.2 left.8.own_ref
  37.9 0.8 copy-done.6
  38.7 0.0 collective-permute-done.4
  38.7 0.0 collective-permute-done.5
  38.7 0.0 collective-permute-done.6
  38.7 14.5 %collective-permute-done.1.yes_ref.rest_0_ = bf16[1024,896]{1,0:T(8,128)(2,1)} collective-permute-done((bf16[1024,896]{1,0:T(8,128)(2,1)}, bf16[1024,896]{1,0:T(8,128)(2,1)}, u32[]{:S(2)}, u32[]{:S(2)}) %collective-permute-start.1) | collective-permute-done | bytes 1835040 | tf_op jit(solution)/shard_map/ppermute | solution.py:301
  53.2 1.5 copy-done.4
  54.7 2.9 %either.1 = bf16[1024,896]{1,0:T(8,128)(2,1)} custom-call(s32[1]{0:T(128)} %bitcast.18.flag_ref, bf16[1024,896]{1,0:T(8,128)(2,1)} %collective-permute-done.1.yes_ref.rest_0_, bf16[1024,896]{1,0:T(8,128)(2,1)S(1)} %copy-done.4), custom_call_target="tpu_custom_call" | custom-call | tf_op jit(solution)/shard_map/either/pallas_call | solution.py:177
  57.7 6.3 %collective-permute-start.14 = (bf16[1024,896]{1,0:T(8,128)(2,1)}, bf16[1024,896]{1,0:T(8,128)(2,1)}, u32[]{:S(2)}, u32[]{:S(2)}) collective-permute-start(bf16[1024,896]{1,0:T(8,128)(2,1)} %either.1), channel_id=1, source_target_pairs={{12,0},{16,28},{0,16},{28,12},{13,1},{17,29},{1,17},{29,13},{14,2}... | collective-permute-start | bytes 5505032 | tf_op jit(solution)/shard_map/ppermute | solution.py:324
  64.0 1.3 collective-permute-start.13
  65.3 0.6 fusion.8
  69.1 0.0 copy-start.9
  69.1 5.5 %collective-permute-start.12 = (bf16[1024,640]{1,0:T(8,128)(2,1)S(1)}, bf16[1024,640]{1,0:T(8,128)(2,1)S(1)}, u32[]{:S(2)}, u32[]{:S(2)}) collective-permute-start(bf16[1024,640]{1,0:T(8,128)(2,1)S(1)} %left.7.own_ref), channel_id=1, source_target_pairs={{0,12},{8,20},{12,24},{16,4},{20,8},{28,16},{1,13},{9,21},{13,25},... | collective-permute-start | bytes 3932168 | tf_op jit(solution)/shard_map/ppermute | solution.py:326
  74.6 1.3 collective-permute-start.8
  75.9 0.0 copy-done.9
  76.0 0.0 copy-start.5
  76.0 0.0 collective-permute-done.9.block_ref
  76.0 3.2 %collective-permute-start.7 = (f32[2,1024]{1,0:T(2,128)S(1)}, f32[2,1024]{1,0:T(2,128)S(1)}, u32[]{:S(2)}, u32[]{:S(2)}) collective-permute-start(f32[2,1024]{1,0:T(2,128)S(1)} %broadcast_multiply_fusion), channel_id=1, source_target_pairs={{0,1},{1,2},{2,3},{4,5},{5,6},{6,7},{8,9},{9,10},{10,11},{12,13},{... | collective-permute-start | bytes 24584 | tf_op jit(solution)/shard_map/ppermute | solution.py:31
  79.2 1.1 held.3.rest_0_
  80.3 0.0 collective-permute-done.7
  80.3 0.0 copy-done.7
  80.3 32.7 %collective-permute-start.10 = (bf16[1024,256]{1,0:T(8,128)(2,1)S(1)}, bf16[1024,256]{1,0:T(8,128)(2,1)S(1)}, u32[]{:S(2)}, u32[]{:S(2)}) collective-permute-start(bf16[1024,256]{1,0:T(8,128)(2,1)S(1)} %copy-done.7), channel_id=1, source_target_pairs={{0,12},{8,20},{12,24},{16,4},{20,8},{28,16},{1,13},{9,21},{13,25},... | collective-permute-start | bytes 1572872 | tf_op jit(solution)/shard_map/ppermute | solution.py:330
  113.0 0.0 collective-permute-done.8
  113.0 1.5 collective-permute-start.11
  114.5 0.6 pad_maximum_fusion.4.factors_ref
  115.1 0.6 slice_bitcast_fusion.3
  115.7 0.0 collective-permute-done.14.rest_1_
  115.8 5.5 %photon.4.rest_2_ = bf16[1,1,2,1024,1024]{4,3,2,1,0:T(8,128)(2,1)} custom-call(f32[4]{0:T(128)S(1)} %pad_maximum_fusion.4.factors_ref, bf16[1,1024,1024]{2,1,0:T(8,128)(2,1)S(1)} %copy-done, f32[1,1024]{1,0:T(1,128)S(1)} %get-tuple-element.36.phonon_ref, bf16[1024,896]{1,0:T(8,128)(2,1)S(1)} %copy-done.5, ...), custom_call_target="tpu_custom_call" | custom-call | tf_op jit(solution)/shard_map/photon/pallas_call | solution.py:263
  121.3 23.5 %collective-permute-done.13.rest_1_ = bf16[1024,896]{1,0:T(8,128)(2,1)} collective-permute-done((bf16[1024,896]{1,0:T(8,128)(2,1)}, bf16[1024,896]{1,0:T(8,128)(2,1)}, u32[]{:S(2)}, u32[]{:S(2)}) %collective-permute-start.13) | collective-permute-done | bytes 1835040 | tf_op jit(solution)/shard_map/ppermute | solution.py:325
  144.7 3.4 %photon.5.rest_2_ = bf16[1,1,2,1024,1024]{4,3,2,1,0:T(8,128)(2,1)} custom-call(f32[4]{0:T(128)S(1)} %pad_maximum_fusion.4.factors_ref, bf16[1,1024,1024]{2,1,0:T(8,128)(2,1)S(1)} %copy-done, f32[1,1024]{1,0:T(1,128)S(1)} %get-tuple-element.36.phonon_ref, bf16[1024,256]{1,0:T(8,128)(2,1)} %left.6.own_ref, ...), custom_call_target="tpu_custom_call", output_to_operand_aliasing={{}: (6, {})} | custom-call | tf_op jit(solution)/shard_map/photon/pallas_call | solution.py:263
  148.1 0.0 collective-permute-done.12.rest_0_
  148.1 4.4 %photon.6.rest_2_ = bf16[1,1,2,1024,1024]{4,3,2,1,0:T(8,128)(2,1)} custom-call(f32[4]{0:T(128)S(1)} %pad_maximum_fusion.4.factors_ref, bf16[1,1024,1024]{2,1,0:T(8,128)(2,1)S(1)} %copy-done, f32[1,1024]{1,0:T(1,128)S(1)} %get-tuple-element.36.phonon_ref, bf16[1024,640]{1,0:T(8,128)(2,1)S(1)} %left.7.own_ref, ...), custom_call_target="tpu_custom_call", output_to_operand_aliasing={{}: (6, {})} | custom-call | tf_op jit(solution)/shard_map/photon/pallas_call | solution.py:263
  152.5 2.1 %collective-permute-done.10.rest_0_ = bf16[1024,256]{1,0:T(8,128)(2,1)S(1)} collective-permute-done((bf16[1024,256]{1,0:T(8,128)(2,1)S(1)}, bf16[1024,256]{1,0:T(8,128)(2,1)S(1)}, u32[]{:S(2)}, u32[]{:S(2)}) %collective-permute-start.10) | collective-permute-done | bytes 524320 | tf_op jit(solution)/shard_map/ppermute | solution.py:330
  154.6 0.0 collective-permute-done.11.rest_1_
  154.6 2.6 %photon.7 = bf16[1,1,2,1024,1024]{4,3,2,1,0:T(8,128)(2,1)} custom-call(f32[4]{0:T(128)S(1)} %pad_maximum_fusion.4.factors_ref, bf16[1,1024,1024]{2,1,0:T(8,128)(2,1)S(1)} %copy-done, f32[1,1024]{1,0:T(1,128)S(1)} %get-tuple-element.36.phonon_ref, bf16[1024,256]{1,0:T(8,128)(2,1)S(1)} %copy-done.7, ...), custom_call_target="tpu_custom_call", output_to_operand_aliasing={{}: (6, {})} | custom-call | tf_op jit(solution)/shard_map/photon/pallas_call | solution.py:263
  (27 shorter events, 0.2 us)
Async XLA Ops:
  0.6 4.9 %copy-start = (bf16[1,1024,1024]{2,1,0:T(8,128)(2,1)S(1)}, bf16[1,1024,1024]{2,1,0:T(8,128)(2,1)}, u32[]{:S(2)}) copy-start(bf16[1,1024,1024]{2,1,0:T(8,128)(2,1)} %dipole_ref.17) | copy-start | bytes 6291460
  0.6 0.8 copy-start.8
  2.5 8.3 %collective-permute-start = (f32[1,2,1024]{2,1,0:T(2,128)S(1)}, f32[1,2,1024]{2,1,0:T(2,128)S(1)}, u32[]{:S(2)}, u32[]{:S(2)}) collective-permute-start(f32[1,2,1024]{2,1,0:T(2,128)S(1)} %diagonals.1), channel_id=1, source_target_pairs={{0,4},{4,0},{8,12},{12,8},{16,20},{20,16},{24,28},{28,24},{1,5},{5... | collective-permute-start | bytes 24584 | tf_op jit(solution)/shard_map/ppermute | solution.py:47
  5.6 6.9 %copy-start.11 = (f32[2,6]{1,0:T(2,128)S(1)}, f32[2,6]{1,0:T(2,128)}, u32[]{:S(2)}) copy-start(f32[2,6]{1,0:T(2,128)} %param.14) | copy-start | bytes 148
  5.6 6.9 %copy-start.12 = (s32[6]{0:T(128)S(1)}, s32[6]{0:T(128)}, u32[]{:S(2)}) copy-start(s32[6]{0:T(128)} %param.13) | copy-start | bytes 76
  9.6 1.2 copy-start.3
  10.9 42.3 %collective-permute-start.1 = (bf16[1024,896]{1,0:T(8,128)(2,1)}, bf16[1024,896]{1,0:T(8,128)(2,1)}, u32[]{:S(2)}, u32[]{:S(2)}) collective-permute-start(bf16[1024,896]{1,0:T(8,128)(2,1)} %copy-done.3), channel_id=1, source_target_pairs={{0,12},{8,20},{12,24},{16,4},{20,8},{28,16},{4,0},{24,28},{1,13},{... | collective-permute-start | bytes 5505032 | tf_op jit(solution)/shard_map/ppermute | solution.py:301
  12.7 0.8 collective-permute-start.2
  13.5 0.7 collective-permute-start.3
  14.5 24.2 %collective-permute-start.4 = (f32[2,1024]{1,0:T(2,128)S(1)}, f32[2,1024]{1,0:T(2,128)S(1)}, u32[]{:S(2)}, u32[]{:S(2)}) collective-permute-start(f32[2,1024]{1,0:T(2,128)S(1)} %get-tuple-element.28), channel_id=1, source_target_pairs={{4,12},{24,16},{5,13},{25,17},{6,14},{26,18},{7,15},{27,19}} | collective-permute-start | bytes 24584 | tf_op jit(solution)/shard_map/ppermute | solution.py:316
  15.1 23.6 %collective-permute-start.5 = (f32[2,1024]{1,0:T(2,128)S(1)}, f32[2,1024]{1,0:T(2,128)S(1)}, u32[]{:S(2)}, u32[]{:S(2)}) collective-permute-start(f32[2,1024]{1,0:T(2,128)S(1)} %get-tuple-element.30), channel_id=1, source_target_pairs={{4,20},{24,8},{5,21},{25,9},{6,22},{26,10},{7,23},{27,11}} | collective-permute-start | bytes 24584 | tf_op jit(solution)/shard_map/ppermute | solution.py:316
  15.8 22.9 %collective-permute-start.6 = (f32[2,1024]{1,0:T(2,128)S(1)}, f32[2,1024]{1,0:T(2,128)S(1)}, u32[]{:S(2)}, u32[]{:S(2)}) collective-permute-start(f32[2,1024]{1,0:T(2,128)S(1)} %get-tuple-element.29), channel_id=1, source_target_pairs={{4,28},{24,0},{5,29},{25,1},{6,30},{26,2},{7,31},{27,3}} | collective-permute-start | bytes 24584 | tf_op jit(solution)/shard_map/ppermute | solution.py:316
  17.1 2.2 %copy-start.1 = (bf16[1,1,2,1024,1024]{4,3,2,1,0:T(8,128)(2,1)S(1)}, bf16[1,1,2,1024,1024]{4,3,2,1,0:T(8,128)(2,1)}, u32[]{:S(2)}) copy-start(bf16[1,1,2,1024,1024]{4,3,2,1,0:T(8,128)(2,1)} %lesser_ref.11) | copy-start | bytes 12582916
  20.8 55.2 %collective-permute-start.9 = (bf16[1024,256]{1,0:T(8,128)(2,1)}, bf16[1024,256]{1,0:T(8,128)(2,1)}, u32[]{:S(2)}, u32[]{:S(2)}) collective-permute-start(bf16[1024,256]{1,0:T(8,128)(2,1)} %left.6.own_ref), channel_id=1, source_target_pairs={{0,12},{8,20},{12,24},{16,4},{20,8},{28,16},{1,13},{9,21},{13,25},... | collective-permute-start | bytes 1572872 | tf_op jit(solution)/shard_map/ppermute | solution.py:302
  29.0 2.2 %copy-start.2 = (bf16[1,1,2,1024,1024]{4,3,2,1,0:T(8,128)(2,1)S(1)}, bf16[1,1,2,1024,1024]{4,3,2,1,0:T(8,128)(2,1)}, u32[]{:S(2)}) copy-start(bf16[1,1,2,1024,1024]{4,3,2,1,0:T(8,128)(2,1)} %lesser_ref.11) | copy-start | bytes 12582916
  37.9 0.8 copy-start.6
  53.2 1.5 copy-start.4
  54.7 10.6 %copy-start.10 = (f32[1,3]{1,0:T(1,128)S(1)}, f32[1,3]{1,0:T(1,128)}, u32[]{:S(2)}) copy-start(f32[1,3]{1,0:T(1,128)} %param.11) | copy-start | bytes 40
  57.7 58.1 %collective-permute-start.14 = (bf16[1024,896]{1,0:T(8,128)(2,1)}, bf16[1024,896]{1,0:T(8,128)(2,1)}, u32[]{:S(2)}, u32[]{:S(2)}) collective-permute-start(bf16[1024,896]{1,0:T(8,128)(2,1)} %either.1), channel_id=1, source_target_pairs={{12,0},{16,28},{0,16},{28,12},{13,1},{17,29},{1,17},{29,13},{14,2}... | collective-permute-start | bytes 5505032 | tf_op jit(solution)/shard_map/ppermute | solution.py:324
  64.0 80.7 %collective-permute-start.13 = (bf16[1024,896]{1,0:T(8,128)(2,1)}, bf16[1024,896]{1,0:T(8,128)(2,1)}, u32[]{:S(2)}, u32[]{:S(2)}) collective-permute-start(bf16[1024,896]{1,0:T(8,128)(2,1)} %left.9), channel_id=1, source_target_pairs={{4,16},{12,0},{16,28},{24,12},{5,17},{13,1},{17,29},{25,13},{6,18}... | collective-permute-start | bytes 5505032 | tf_op jit(solution)/shard_map/ppermute | solution.py:325
  69.1 6.9 %copy-start.9 = (f32[1,1024]{1,0:T(1,128)S(1)}, f32[1,1024]{1,0:T(1,128)}, u32[]{:S(2)}) copy-start(f32[1,1024]{1,0:T(1,128)} %param.15) | copy-start | bytes 12292
  69.1 79.0 %collective-permute-start.12 = (bf16[1024,640]{1,0:T(8,128)(2,1)S(1)}, bf16[1024,640]{1,0:T(8,128)(2,1)S(1)}, u32[]{:S(2)}, u32[]{:S(2)}) collective-permute-start(bf16[1024,640]{1,0:T(8,128)(2,1)S(1)} %left.7.own_ref), channel_id=1, source_target_pairs={{0,12},{8,20},{12,24},{16,4},{20,8},{28,16},{1,13},{9,21},{13,25},... | collective-permute-start | bytes 3932168 | tf_op jit(solution)/shard_map/ppermute | solution.py:326
  74.6 38.4 %collective-permute-start.8 = (f32[2,1024]{1,0:T(2,128)S(1)}, f32[2,1024]{1,0:T(2,128)S(1)}, u32[]{:S(2)}, u32[]{:S(2)}) collective-permute-start(f32[2,1024]{1,0:T(2,128)S(1)} %held.2), channel_id=1, source_target_pairs={{1,0},{2,1},{3,2},{5,4},{6,5},{7,6},{9,8},{10,9},{11,10},{13,12},{... | collective-permute-start | bytes 24584 | tf_op jit(solution)/shard_map/ppermute | solution.py:31
  76.0 4.3 %copy-start.7 = (bf16[1024,256]{1,0:T(8,128)(2,1)S(1)}, bf16[1024,256]{1,0:T(8,128)(2,1)}, u32[]{:S(2)}) copy-start(bf16[1024,256]{1,0:T(8,128)(2,1)} %copy-done.6) | copy-start | bytes 1572868
  76.0 39.8 %copy-start.5 = (bf16[1024,896]{1,0:T(8,128)(2,1)S(1)}, bf16[1024,896]{1,0:T(8,128)(2,1)}, u32[]{:S(2)}) copy-start(bf16[1024,896]{1,0:T(8,128)(2,1)} %copy-done.3) | copy-start | bytes 5505028
  76.0 4.3 %collective-permute-start.7 = (f32[2,1024]{1,0:T(2,128)S(1)}, f32[2,1024]{1,0:T(2,128)S(1)}, u32[]{:S(2)}, u32[]{:S(2)}) collective-permute-start(f32[2,1024]{1,0:T(2,128)S(1)} %broadcast_multiply_fusion), channel_id=1, source_target_pairs={{0,1},{1,2},{2,3},{4,5},{5,6},{6,7},{8,9},{9,10},{10,11},{12,13},{... | collective-permute-start | bytes 24584 | tf_op jit(solution)/shard_map/ppermute | solution.py:31
  80.3 74.3 %collective-permute-start.10 = (bf16[1024,256]{1,0:T(8,128)(2,1)S(1)}, bf16[1024,256]{1,0:T(8,128)(2,1)S(1)}, u32[]{:S(2)}, u32[]{:S(2)}) collective-permute-start(bf16[1024,256]{1,0:T(8,128)(2,1)S(1)} %copy-done.7), channel_id=1, source_target_pairs={{0,12},{8,20},{12,24},{16,4},{20,8},{28,16},{1,13},{9,21},{13,25},... | collective-permute-start | bytes 1572872 | tf_op jit(solution)/shard_map/ppermute | solution.py:330
  113.0 41.6 %collective-permute-start.11 = (bf16[1024,256]{1,0:T(8,128)(2,1)S(1)}, bf16[1024,256]{1,0:T(8,128)(2,1)S(1)}, u32[]{:S(2)}, u32[]{:S(2)}) collective-permute-start(bf16[1024,256]{1,0:T(8,128)(2,1)S(1)} %copy-done.7), channel_id=1, source_target_pairs={{4,16},{12,0},{16,28},{24,12},{5,17},{13,1},{17,29},{25,13},{6,18}... | collective-permute-start | bytes 1572872 | tf_op jit(solution)/shard_map/ppermute | solution.py:329
